TPU v7x, 768 devices: a whole 4x8x12 slice. The times are simulated.
768 devices in a mesh: dp: 64 (over x, y, core), table: 12 (over z).
Axes of the slice: x: 4, y: 8, z: 12, core: 2. Of those that a mesh axis runs over, the one named last changes fastest.
Arguments:
- dense_input: bfloat16 [98304, 13], P(('dp', 'table')), may hold values from -6 to 6
- hot_ids: int32 [98304, 52], P(('dp', 'table')), may hold values from 0 to 3071
- logit_grad: float32 [98304], P(('dp', 'table')), may hold values from -0.875 to 0.875
- hot_table: bfloat16 [3072, 128], replicated, may hold values from -6 to 6
- hot_accum: float32 [3072], replicated, may hold values from 0.03 to 1
- cold_table: bfloat16 [393216, 128], P(('dp', 'table')), may hold values from -6 to 6
- cold_accum: float32 [393216], P(('dp', 'table')), may hold values from 3.90625e-06 to 0.00013020834
- send_rows: int32 [9216, 256], P(('dp', 'table')), may hold values from 0 to 511
- send_count: int32 [768, 12], P(('dp', 'table')), may hold values from 1 to 256, as said below
- recv_bags: int32 [9216, 256], P(('dp', 'table')), may hold values from 0 to 3327
- bottom_one: bfloat16 [13, 512], replicated, may hold values from -1.75 to 1.75
- bottom_two: bfloat16 [512, 256], replicated, may hold values from -0.25 to 0.25
- bottom_three: bfloat16 [256, 128], replicated, may hold values from -0.375 to 0.375
- cross_down: bfloat16 [3456, 512], replicated, may hold values from -0.109375 to 0.109375
- cross_up: bfloat16 [512, 3456], replicated, may hold values from -0.25 to 0.25
- head_vector: float32 [3456], replicated, may hold values from -0.109375 to 0.109375
Outputs:
- logits: float32 [98304], P(('dp', 'table'))
- new_hot: float32 [3072, 128], replicated
- new_cold: float32 [393216, 128], P(('dp', 'table'))
Inputs may be any that keep to these rules, and one draw needn't show every extreme that they name: `send_count`: live slots of an owner to one sample owner; in every draw some owner fills all 256 slots to some sample owner, and owners' loads differ by up to four times.
All inputs are finite; a program needn't handle non-finite values.
Results may differ from a plain program's by a relative error of at most 0.0046.
Values may be sent and summed in bfloat16 or wider, within the bound.
No kernel may reach another device: no remote copies, remote signals or barrier semaphores. Data moves between devices by JAX's collectives and lax.ppermute only.
A program may use at most 64 MiB of HBM per device.

v0:
```python
import jax
import jax.numpy as jnp
from jax import lax
from jax.sharding import PartitionSpec as P

E = 128
TABLES = 26
LH = 2
HOT = 3072


def forward_backward(
    features,
    hot_index,
    cold_pool,
    hot_table,
    bottom_one,
    bottom_two,
    bottom_three,
    cross_down,
    cross_up,
    head_vector,
    upstream_grad,
):
    samples = features.shape[0]
    first_act = jax.nn.relu(
        jnp.dot(features, bottom_one, preferred_element_type=jnp.float32)
    ).astype(jnp.bfloat16)
    second_act = jax.nn.relu(
        jnp.dot(first_act, bottom_two, preferred_element_type=jnp.float32)
    ).astype(jnp.bfloat16)
    bottom_out = jax.nn.relu(jnp.dot(second_act, bottom_three, preferred_element_type=jnp.float32))
    looked_up = hot_table[hot_index].astype(jnp.float32).reshape(samples, TABLES, LH, E).sum(axis=2)
    pooled = looked_up + cold_pool.reshape(samples, TABLES, E)
    inputs_cross = jnp.concatenate(
        [bottom_out, pooled.reshape(samples, TABLES * E)], axis=1
    ).astype(jnp.bfloat16)
    lowrank = jnp.dot(inputs_cross, cross_down, preferred_element_type=jnp.float32).astype(
        jnp.bfloat16
    )
    crossed = jnp.dot(lowrank, cross_up, preferred_element_type=jnp.float32)
    widened = inputs_cross.astype(jnp.float32)
    gated = crossed + 1.0
    logits = jnp.sum(widened * gated * head_vector[None, :], axis=1)
    outer_grad = upstream_grad[:, None] * head_vector[None, :]
    cross_grad = (outer_grad * widened).astype(jnp.bfloat16)
    lowrank_grad = lax.dot_general(
        cross_grad, cross_up, (((1,), (1,)), ((), ())), preferred_element_type=jnp.float32
    ).astype(jnp.bfloat16)
    input_grad = outer_grad * gated + lax.dot_general(
        lowrank_grad, cross_down, (((1,), (1,)), ((), ())), preferred_element_type=jnp.float32
    )
    bag_grad = input_grad[:, E:].astype(jnp.bfloat16).reshape(samples, TABLES, E)
    return (logits, bag_grad)


def adagrad_rows(table_rows, accum_rows, gradient):
    updated_accum = accum_rows + jnp.mean(gradient * gradient, axis=1)
    return table_rows.astype(jnp.float32) - 1.0 * gradient / jnp.sqrt(updated_accum)[:, None]


def body(
    dense_input,
    hot_ids,
    logit_grad,
    hot_table,
    hot_accum,
    cold_table,
    cold_accum,
    send_rows,
    send_count,
    recv_bags,
    bottom_one,
    bottom_two,
    bottom_three,
    cross_down,
    cross_up,
    head_vector,
):
    samples = dense_input.shape[0]
    owned_rows = cold_table.shape[0]
    slot_total = send_rows.shape[1]
    alive = lax.iota(jnp.int32, slot_total)[None, :] < send_count[0][:, None]
    picked = cold_table[send_rows]
    outgoing = jnp.where(alive[:, :, None], picked, jnp.zeros_like(picked))
    arrived = lax.all_to_all(outgoing, "table", split_axis=0, concat_axis=0, tiled=True)
    bag_index = recv_bags.reshape(-1)
    cold_pool = jax.ops.segment_sum(
        arrived.reshape(-1, E).astype(jnp.float32), bag_index, num_segments=samples * TABLES
    )
    logits, bag_grad = forward_backward(
        dense_input,
        hot_ids,
        cold_pool,
        hot_table,
        bottom_one,
        bottom_two,
        bottom_three,
        cross_down,
        cross_up,
        head_vector,
        logit_grad,
    )
    slot_grad = bag_grad.reshape(-1, E)[recv_bags]
    returned = lax.all_to_all(slot_grad, "table", split_axis=0, concat_axis=0, tiled=True)
    masked = jnp.where(alive[:, :, None], returned.astype(jnp.float32), 0.0)
    cold_grad = jax.ops.segment_sum(
        masked.reshape(-1, E), send_rows.reshape(-1), num_segments=owned_rows
    )
    new_cold = adagrad_rows(cold_table, cold_accum, cold_grad)
    spread = jnp.broadcast_to(
        bag_grad[:, :, None, :].astype(jnp.float32), (samples, TABLES, LH, E)
    ).reshape(-1, E)
    hot_local = jax.ops.segment_sum(spread, hot_ids.reshape(-1), num_segments=HOT)
    hot_grad = lax.psum(hot_local, ("dp", "table"))
    new_hot = adagrad_rows(hot_table, hot_accum, hot_grad)
    return (logits, new_hot, new_cold)


def solution(mesh):
    return jax.shard_map(
        body,
        mesh=mesh,
        in_specs=(
            P(("dp", "table"), None),
            P(("dp", "table"), None),
            P(("dp", "table")),
            P(),
            P(),
            P(("dp", "table"), None),
            P(("dp", "table")),
            P(("dp", "table"), None),
            P(("dp", "table"), None),
            P(("dp", "table"), None),
            P(),
            P(),
            P(),
            P(),
            P(),
            P(),
        ),
        out_specs=(P(("dp", "table")), P(), P(("dp", "table"), None)),
        check_vma=False,
    )
```

profile of v0, /device:TPU:1, one launch (start us, length us, event | category | flops | bytes accessed | tf_op | source)
XLA Modules:
  0.0 707.9 jit_solution(14623481674302101247)
XLA Ops:
  7.2 1.5 iota_compare_fusion
  8.6 0.7 compare_select_fusion.2
  9.4 0.6 reshape.78
  10.0 0.7 broadcast_clamp_fusion.1
  10.7 12.0 %gather_fusion.1 = bf16[3072,128]{1,0:T(8,128)(2,1)} fusion(bf16[512,128]{1,0:T(8,128)(2,1)} %param.21, s32[3072]{0:T(1024)S(1)} %broadcast_clamp_fusion.1), kind=kCustom, calls=%fused_computation.1 | custom fusion | bytes 1585152 | tf_op jit(solution)/shard_map/gather | solution.py:84
  22.6 2.3 broadcast_select_fusion
  25.0 15.7 %all-to-all-start = ((bf16[12,256,128]{2,1,0:T(8,128)(2,1)}), bf16[12,256,128]{2,1,0:T(8,128)(2,1)}, u32[]{:S(2)}, u32[]{:S(2)}) async-start(bf16[12,256,128]{2,1,0:T(8,128)(2,1)} %broadcast_select_fusion), calls=%async_computation | async-start | bytes 1572864 | tf_op jit(solution)/shard_map/all_to_all | solution.py:86
  40.7 0.6 reshape.94
  41.3 1.4 compare_select_fusion
  42.7 1.5 copy.26
  44.1 1.5 reshape.70
  45.7 1.4 pad_clamp_fusion
  47.0 15.4 %gather_fusion = bf16[6656,128]{1,0:T(8,128)(2,1)} fusion(bf16[3072,128]{1,0:T(8,128)(2,1)} %param.19, s32[7168]{0:T(1024)} %pad_clamp_fusion), kind=kCustom, calls=%fused_computation | custom fusion | bytes 3434496 | tf_op jit(solution)/shard_map/gather | solution.py:33
  62.4 7.6 %convert_reduce_fusion = f32[128,26,128]{2,1,0:T(8,128)} fusion(bf16[128,26,2,128]{3,2,1,0:T(2,128)(2,1)} %bitcast.20), kind=kLoop, calls=%fused_computation.7 | loop fusion | flops 1277952 | bytes 3407872 | tf_op jit(solution)/shard_map/reduce_sum | solution.py:33
  70.0 2.8 copy.27
  72.8 2.7 copy.28
  75.5 2.0 fusion.10
  77.4 1.7 fusion.11
  79.1 1.5 copy.29
  80.6 0.6 compare_select_fusion.1
  81.2 1.3 reshape.86
  82.5 0.7 broadcast_clamp_fusion
  83.2 18.5 %scatter_custom_fusion = f32[3328,128]{1,0:T(8,128)} fusion(s32[3072]{0:T(1024)} %reshape.94, bf16[3072,128]{1,0:T(8,128)(2,1)} %bitcast.10, f32[]{:T(128)} %constant.8.clone.1), kind=kCustom, calls=%fused_computation.17 | custom fusion | flops 786432 | bytes 2490880 | tf_op jit(solution)/shard_map/scatter-add | solution.py:88
  101.8 2.6 reshape.62
  104.4 3.0 add_convert_fusion
  107.4 6.1 broadcast_multiply_fusion
  113.5 5.8 fusion.9
  119.3 3.6 fusion.3
  122.9 2.9 reshape_reshape.3
  125.8 12.2 %gather_fusion.2 = bf16[3072,128]{1,0:T(8,128)(2,1)} fusion(bf16[3328,128]{1,0:T(8,128)(2,1)} %reshape_reshape.3, s32[3072]{0:T(1024)S(1)} %broadcast_clamp_fusion), kind=kCustom, calls=%fused_computation.2 | custom fusion | bytes 1585152 | tf_op jit(solution)/shard_map/gather | solution.py:104
  138.0 9.0 %all-to-all-start.1 = ((bf16[12,256,128]{2,1,0:T(8,128)(2,1)}), bf16[12,256,128]{2,1,0:T(8,128)(2,1)}, u32[]{:S(2)}, u32[]{:S(2)}) async-start(bf16[12,256,128]{2,1,0:T(8,128)(2,1)} %bitcast.24), calls=%async_computation.1 | async-start | bytes 1572864 | tf_op jit(solution)/shard_map/all_to_all | solution.py:105
  147.1 0.0 all-reduce.2.cloned.1.call-start
  147.1 1.5 copy.30
  148.6 1.5 reshape.102
  150.1 2.4 copy.31
  152.5 3.1 copy.32
  155.7 4.6 broadcast_in_dim.58
  160.3 37.4 %scatter_custom_fusion.1 = f32[3072,128]{1,0:T(8,128)} fusion(s32[6656]{0:T(1024)} %reshape.102, f32[6656,128]{1,0:T(8,128)} %bitcast.23, f32[]{:T(128)} %constant.8.clone.1), kind=kCustom, calls=%fused_computation.35 | custom fusion | flops 851968 | bytes 1573376 | tf_op jit(solution)/shard_map/scatter-add | solution.py:114
  197.7 0.0 all-reduce.2.cloned.1.call-update
  197.7 0.6 reshape.110
  198.3 473.6 %all-reduce.2.cloned.1.call-done = f32[3072,128]{1,0:T(8,128)} async-done(((f32[3072,128]{1,0:T(8,128)}), f32[3072,128]{1,0:T(8,128)}) %all-reduce.2.cloned.1.call-update) | async-done | bytes 1572880 | tf_op jit(solution)/shard_map/psum | solution.py:115
  671.9 2.0 multiply_reduce_fusion
  673.9 0.7 add_sqrt_fusion
  674.6 3.1 divide_subtract_fusion
  677.7 2.5 convert_select_fusion
  680.2 17.9 %scatter_custom_fusion.2 = f32[512,128]{1,0:T(8,128)} fusion(s32[3072]{0:T(1024)} %reshape.110, f32[3072,128]{1,0:T(8,128)} %bitcast.26, f32[]{:T(128)} %constant.8.clone.1), kind=kCustom, calls=%fused_computation.40 | custom fusion | flops 393216 | bytes 262656 | tf_op jit(solution)/shard_map/scatter-add | solution.py:107
  698.1 1.1 multiply_reduce_fusion.1
  699.2 1.8 divide_subtract_fusion.1
  (17 shorter events, 0.0 us)
Async XLA Ops:
  7.2 100.3 %copy-start = (bf16[512,3456]{1,0:T(8,128)(2,1)S(1)}, bf16[512,3456]{1,0:T(8,128)(2,1)}, u32[]{:S(2)}) copy-start(bf16[512,3456]{1,0:T(8,128)(2,1)} %param.30) | copy-start | bytes 10616836
  22.6 18.1 %copy-start.2 = (s32[12,256]{1,0:T(8,128)S(1)}, s32[12,256]{1,0:T(8,128)}, u32[]{:S(2)}) copy-start(s32[12,256]{1,0:T(8,128)} %param.25) | copy-start | bytes 36868
  25.0 58.3 %all-to-all-start = ((bf16[12,256,128]{2,1,0:T(8,128)(2,1)}), bf16[12,256,128]{2,1,0:T(8,128)(2,1)}, u32[]{:S(2)}, u32[]{:S(2)}) async-start(bf16[12,256,128]{2,1,0:T(8,128)(2,1)} %broadcast_select_fusion), calls=%async_computation | async-start | bytes 1572864 | tf_op jit(solution)/shard_map/all_to_all | solution.py:86
  104.4 3.0 copy-start.5
  138.0 539.7 %all-to-all-start.1 = ((bf16[12,256,128]{2,1,0:T(8,128)(2,1)}), bf16[12,256,128]{2,1,0:T(8,128)(2,1)}, u32[]{:S(2)}, u32[]{:S(2)}) async-start(bf16[12,256,128]{2,1,0:T(8,128)(2,1)} %bitcast.24), calls=%async_computation.1 | async-start | bytes 1572864 | tf_op jit(solution)/shard_map/all_to_all | solution.py:105
  147.1 524.8 %all-reduce.2.cloned.1.call-start = ((), (), s32[]{:S(2)}) async-start(), calls=%async_computation.2 | async-start | bytes 3145728 | tf_op jit(solution)/shard_map/psum | solution.py:115
  160.3 37.4 %copy-start.3 = (s32[12,256]{1,0:T(8,128)S(1)}, s32[12,256]{1,0:T(8,128)}, u32[]{:S(2)}) copy-start(s32[12,256]{1,0:T(8,128)} %param.23) | copy-start | bytes 36868
  671.9 2.7 copy-start.1
  674.6 3.1 copy-start.4
  677.7 21.5 %copy-start.6 = (f32[512]{0:T(512)S(1)}, f32[512]{0:T(512)}, u32[]{:S(2)}) copy-start(f32[512]{0:T(512)} %param.22) | copy-start | bytes 6148
Sparse Core Ops, SparseCore 0:
  197.8 474.0 all-reduce.1
where the time goes:
time: 710 us; the launch traced here: 708 us
  waiting for transfers between devices  474 us (67%)
  other arithmetic  108 us (15%)
  local copies, waits for them, and re-layouts  71.3 us (10%)
  starting transfers between devices  24.8 us (3%)
  matrix products  15.6 us (2%)
  between operations  14.1 us (2%)
    psum x1, waiting for transfers between devices, body(): hot_grad = lax.psum(hot_local, ('dp', 'table'))  474 us
    scatter-add x1, other arithmetic, body(): jax.ops.segment_sum(spread, hot_ids.reshape(-1), num_segments=HOT)  37.4 us
    scatter-add x1, other arithmetic, body(): jax.ops.segment_sum(arrived.reshape(-1, E).astype(jnp.float32), bag_index...  18.5 us
    scatter-add x1, other arithmetic, body(): jax.ops.segment_sum(masked.reshape(-1, E), send_rows.reshape(-1), num_seg...  17.9 us
    all_to_all x1, starting transfers between devices, body(): lax.all_to_all(outgoing, 'table', split_axis=0, concat_axis=0, tiled=True)  15.7 us
    gather x1, local copies, waits for them, and re-layouts, forward_backward(): hot_table[hot_index].astype(jnp.float32).reshape(samples, TABLES, LH, E)  15.4 us
  transfers between devices with their start and end apart: 3, of which 1 were waited for; matrix products, arithmetic and copies ran while one was open for 14% of the time, Pallas kernels for 0%

commit v1 on v0

v1 whole, which is shorter than its diff:
```python
import jax
import jax.numpy as jnp
from jax import lax
from jax.experimental import pallas as pl
from jax.experimental.pallas import tpu as pltpu
from jax.sharding import PartitionSpec as P

E = 128
TABLES = 26
HALF = 13
LH = 2
HOT = 3072
B = 128
ROWS = 512
CAP = 256
NT = 12
SLOTS = NT * CAP
BAGS = B * TABLES
HB = B * HALF
R = 512
F = 3456
f32 = jnp.float32
bf = jnp.bfloat16
VLIM = 56 * 1024 * 1024
VM = pl.BlockSpec(memory_space=pltpu.VMEM)
SM = pl.BlockSpec(memory_space=pltpu.SMEM)
ANY = pl.BlockSpec(memory_space=pl.ANY)


def dot(a, b):
    return jnp.dot(a, b, preferred_element_type=f32)


def dot_t(a, b):
    return lax.dot_general(a, b, (((1,), (1,)), ((), ())), preferred_element_type=f32)


def hit(idx, base, shape, axis):
    place = lax.broadcasted_iota(jnp.int32, shape, axis)
    return jnp.where(idx - base == place, 1.0, 0.0).astype(bf)


def call(kernel, outs, n_in_specs, scratch=(), flops=0, nbytes=0):
    return pl.pallas_call(
        kernel,
        out_shape=outs,
        in_specs=n_in_specs,
        out_specs=jax.tree.map(lambda _: VM, outs),
        scratch_shapes=list(scratch),
        compiler_params=pltpu.CompilerParams(vmem_limit_bytes=VLIM),
        cost_estimate=pl.CostEstimate(flops=flops, bytes_accessed=nbytes, transcendentals=0),
    )


def split_bag(bag):
    sample = (bag * 2521) >> 16
    table = bag - sample * TABLES
    upper = table >= HALF
    return upper, jnp.where(upper, table - HALF, table) * B + sample


def pick_kernel(count_ref, rows_ref, table_ref, out_ref, wide):
    wide[:, :E] = table_ref[: ROWS // 2, :]
    wide[:, E:] = table_ref[ROWS // 2 :, :]
    slot = lax.broadcasted_iota(jnp.int32, (CAP, 1), 0)
    for s in range(NT):
        row = rows_ref[:, s : s + 1]
        row = jnp.where(slot < count_ref[0, s], row, -1)
        upper = row >= ROWS // 2
        low = jnp.where(upper, row - ROWS // 2, row)
        both = dot(hit(low, 0, (CAP, ROWS // 2), 1), wide[...])
        out_ref[s * CAP : (s + 1) * CAP, :] = jnp.where(upper, both[:, E:], both[:, :E]).astype(bf)


def hot_kernel(ids_ref, table_ref, dense_ref, one_ref, two_ref, three_ref, out_ref, bottom_ref):
    first = jnp.maximum(dot(dense_ref[...], one_ref[...]), 0.0).astype(bf)
    second = jnp.maximum(dot(first, two_ref[...]), 0.0).astype(bf)
    bottom_ref[...] = jnp.maximum(dot(second, three_ref[...]), 0.0).astype(bf)

    def pair(j, _):
        ids = pltpu.roll(ids_ref[...], lax.rem(128 - 4 * j, 128), 1)
        left = jnp.concatenate([ids[:, 0:1], ids[:, 2:3]], axis=0)
        right = jnp.concatenate([ids[:, 1:2], ids[:, 3:4]], axis=0)
        count = hit(left, 0, (2 * B, HOT), 1) + hit(right, 0, (2 * B, HOT), 1)
        out_ref[pl.ds(pl.multiple_of(j * 2 * B, 2 * B), 2 * B), :] = dot(count, table_ref[...])
        return 0

    lax.fori_loop(0, HALF, pair, 0)


M_POOL = 416


def cross_kernel(
    hot_ref,
    bottom_ref,
    arrived_ref,
    bags_ref,
    bags_t_ref,
    grad_ref,
    head_ref,
    down_hbm,
    up_hbm,
    logits_ref,
    bag_grad_ref,
    slot_ref,
    down,
    up,
    wide,
    cold,
    x0,
    sems,
):
    copy_down = pltpu.make_async_copy(down_hbm, down, sems.at[0])
    copy_up = pltpu.make_async_copy(up_hbm, up, sems.at[1])
    copy_down.start()
    copy_up.start()
    zero = jnp.zeros((CAP, E), bf)
    for s in range(NT):
        upper, _ = split_bag(bags_t_ref[:, s : s + 1])
        block = arrived_ref[s * CAP : (s + 1) * CAP, :]
        wide[s * CAP : (s + 1) * CAP, :E] = jnp.where(upper, zero, block)
        wide[s * CAP : (s + 1) * CAP, E:] = jnp.where(upper, block, zero)
    _, place = split_bag(bags_ref[...])

    def pool(j, _):
        base = j * M_POOL
        flat = jnp.concatenate([place[s : s + 1, :] for s in range(NT)], axis=1)
        part = dot(hit(flat, base, (M_POOL, SLOTS), 0), wide[...])
        cold[pl.ds(pl.multiple_of(base, M_POOL), M_POOL), :] = part
        return 0

    lax.fori_loop(0, HB // M_POOL, pool, 0)
    x0[:, :E] = bottom_ref[...]
    for t in range(TABLES):
        r = (t % HALF) * B
        c = (t // HALF) * E
        x0[:, E * (t + 1) : E * (t + 2)] = (
            hot_ref[t * B : (t + 1) * B, :] + cold[r : r + B, c : c + E]
        ).astype(bf)
    copy_down.wait()
    copy_up.wait()
    low = dot(x0[...], down[...]).astype(bf)
    upstream = grad_ref[...]
    total = jnp.zeros((B, E), f32)
    low_grad = jnp.zeros((B, R), f32)
    for k in range(TABLES + 1):
        cols = slice(E * k, E * (k + 1))
        head = head_ref[:, cols]
        wide_x = x0[:, cols].astype(f32)
        gated = dot(low, up[:, cols]) + 1.0
        total = total + wide_x * gated * head
        outer = upstream * head
        low_grad = low_grad + dot_t((outer * wide_x).astype(bf), up[:, cols])
        if k > 0:
            t = k - 1
            r = (t % HALF) * B
            c = (t // HALF) * E
            cold[r : r + B, c : c + E] = outer * gated
    logits_ref[...] = jnp.sum(total, axis=1, keepdims=True)
    low_grad = low_grad.astype(bf)
    for t in range(TABLES):
        r = (t % HALF) * B
        c = (t // HALF) * E
        part = dot_t(low_grad, down[E * (t + 1) : E * (t + 2), :])
        bag_grad_ref[r : r + B, c : c + E] = (cold[r : r + B, c : c + E] + part).astype(bf)


def slot_kernel(bags_t_ref, bag_grad_ref, slot_ref):
    for s in range(NT):
        upper, place_s = split_bag(bags_t_ref[:, s : s + 1])
        both = dot(hit(place_s, 0, (CAP, HB), 1), bag_grad_ref[...])
        slot_ref[s * CAP : (s + 1) * CAP, :] = jnp.where(upper, both[:, E:], both[:, :E]).astype(bf)


M_HOT = 256


def hot_grad_kernel(ids_t_ref, bag_grad_ref, out_ref, stack):
    for t in range(TABLES):
        r = (t % HALF) * B
        c = (t // HALF) * E
        stack[t * B : (t + 1) * B, :] = bag_grad_ref[r : r + B, c : c + E]
    left = jnp.concatenate([ids_t_ref[2 * t : 2 * t + 1, :] for t in range(TABLES)], axis=1)
    right = jnp.concatenate([ids_t_ref[2 * t + 1 : 2 * t + 2, :] for t in range(TABLES)], axis=1)

    def rows(j, _):
        base = j * M_HOT
        count = hit(left, base, (M_HOT, BAGS), 0) + hit(right, base, (M_HOT, BAGS), 0)
        out_ref[pl.ds(pl.multiple_of(base, M_HOT), M_HOT), :] = dot(count, stack[...])
        return 0

    lax.fori_loop(0, HOT // M_HOT, rows, 0)


def cold_kernel(count_ref, rows_ref, returned_ref, table_ref, accum_ref, out_ref):
    lane = lax.broadcasted_iota(jnp.int32, (1, CAP), 1)
    flat = jnp.concatenate(
        [jnp.where(lane < count_ref[0, s], rows_ref[s : s + 1, :], -1) for s in range(NT)], axis=1
    )
    grad = dot(hit(flat, 0, (ROWS, SLOTS), 0), returned_ref[...])
    updated = accum_ref[...] + jnp.mean(grad * grad, axis=1, keepdims=True)
    out_ref[...] = table_ref[...].astype(f32) - grad / jnp.sqrt(updated)


def sds(shape, dtype):
    return jax.ShapeDtypeStruct(shape, dtype)


def pick(count, rows_t, table):
    return call(pick_kernel, sds((SLOTS, E), bf), [SM, VM, VM], [pltpu.VMEM((ROWS // 2, 2 * E), bf)], 2 * SLOTS * ROWS * E, 2000000)(
        count, rows_t, table
    )


def hot_pool(ids, table, dense, one, two, three):
    return call(hot_kernel, (sds((BAGS, E), f32), sds((B, E), bf)), [VM] * 6, (), 2 * BAGS * HOT * E, 4000000)(
        ids, table, dense, one, two, three
    )


def cross(hot, bottom, arrived, bags, bags_t, grad, head, down, up):
    def kernel(*refs):
        cross_kernel(*refs[:11], None, *refs[11:])

    return call(
        kernel,
        (sds((B, 1), f32), sds((HB, 2 * E), bf)),
        [VM] * 7 + [ANY] * 2,
        [
            pltpu.VMEM((F, R), bf),
            pltpu.VMEM((R, F), bf),
            pltpu.VMEM((SLOTS, 2 * E), bf),
            pltpu.VMEM((HB, 2 * E), f32),
            pltpu.VMEM((B, F), bf),
            pltpu.SemaphoreType.DMA((2,)),
        ],
        2 * BAGS * SLOTS * E + 8 * B * F * R,
        12000000,
    )(hot, bottom, arrived, bags, bags_t, grad, head, down, up)


def slot_grads(bags_t, bag_grad):
    return call(slot_kernel, sds((SLOTS, E), bf), [VM] * 2, (), 2 * BAGS * SLOTS * E, 2000000)(bags_t, bag_grad)


def hot_sum(ids_t, bag_grad):
    return call(hot_grad_kernel, sds((HOT, E), f32), [VM] * 2, [pltpu.VMEM((BAGS, E), bf)], 2 * BAGS * HOT * E, 3000000)(ids_t, bag_grad)


def cold_update(count, rows, returned, table, accum):
    return call(cold_kernel, sds((ROWS, E), f32), [SM] + [VM] * 4, (), 2 * ROWS * SLOTS * E, 2000000)(
        count, rows, returned, table, accum
    )


def a2a(v, axis, groups=None):
    return lax.all_to_all(v, axis, split_axis=0, concat_axis=0, tiled=True, axis_index_groups=groups)


def body(
    dense_input,
    hot_ids,
    logit_grad,
    hot_table,
    hot_accum,
    cold_table,
    cold_accum,
    send_rows,
    send_count,
    recv_bags,
    bottom_one,
    bottom_two,
    bottom_three,
    cross_down,
    cross_up,
    head_vector,
):
    n_dp = lax.axis_size("dp")
    n_xy = n_dp // 2
    xy_groups = [[2 * k + c for k in range(n_xy)] for c in range(2)]
    twin = [(i, i ^ 1) for i in range(n_dp)]
    outgoing = pick(send_count, send_rows.T, cold_table)
    arrived = a2a(outgoing, "table")
    bags_t = recv_bags.T
    ids = jnp.pad(hot_ids, ((0, 0), (0, 128 - TABLES * LH)))
    hot, bottom = hot_pool(ids, hot_table, dense_input, bottom_one, bottom_two, bottom_three)
    logits, bag_grad = cross(
        hot, bottom, arrived, recv_bags, bags_t, logit_grad[:, None], head_vector[None, :], cross_down, cross_up
    )
    hot_local = hot_sum(hot_ids.T, bag_grad)
    core = lax.rem(lax.axis_index("dp"), 2)
    half = HOT // 2
    mine = lax.dynamic_slice_in_dim(hot_local, core * half, half, 0)
    other = lax.dynamic_slice_in_dim(hot_local, (1 - core) * half, half, 0).astype(bf)
    met = lax.ppermute(other, "dp", twin)
    slot_grad = slot_grads(bags_t, bag_grad)
    returned = a2a(slot_grad, "table")
    chip = (mine + met.astype(f32)).astype(bf)
    share = half // n_xy
    plane = a2a(chip, "dp", xy_groups)
    plane = jnp.sum(plane.reshape(n_xy, share, E).astype(f32), axis=0).astype(bf)
    column = a2a(jnp.broadcast_to(plane[None], (NT, share, E)).reshape(NT * share, E), "table")
    grad = jnp.sum(column.reshape(NT, share, E).astype(f32), axis=0)
    first = core * half + lax.div(lax.axis_index("dp"), 2) * share
    accum = lax.dynamic_slice_in_dim(hot_accum, first, share, 0)
    step = grad / jnp.sqrt(accum + jnp.mean(grad * grad, axis=1))[:, None]
    step = step.astype(bf)
    steps = a2a(jnp.broadcast_to(step[None], (n_xy, share, E)).reshape(half, E), "dp", xy_groups)
    others = lax.ppermute(steps, "dp", twin)
    low = jnp.where(core == 0, steps, others)
    high = jnp.where(core == 0, others, steps)
    new_hot = hot_table.astype(f32) - jnp.concatenate([low, high], axis=0).astype(f32)
    new_cold = cold_update(send_count, send_rows, returned, cold_table, cold_accum[:, None])
    return (logits[:, 0], new_hot, new_cold)


def solution(mesh):
    rows = P(("dp", "table"), None)
    flat = P(("dp", "table"))
    return jax.shard_map(
        body,
        mesh=mesh,
        in_specs=(rows, rows, flat, P(), P(), rows, flat, rows, rows, rows, P(), P(), P(), P(), P(), P()),
        out_specs=(flat, P(), rows),
        check_vma=False,
    )
```

time: 710 us -> 188 us (0.26)
  the two profiles are of different devices: /device:TPU:1 before, /device:TPU:8 now
where the time goes in v1:
time: 188 us; the launch traced here: 187 us
  waiting for transfers between devices  59.2 us (31%)
  Pallas kernels  54.4 us (29%)
  starting transfers between devices  32.9 us (18%)
  blocking collectives  25.3 us (13%)
  local copies, waits for them, and re-layouts  10.4 us (6%)
  other arithmetic  4.29 us (2%)
    all_to_all x4, waiting for transfers between devices, a2a(): lax.all_to_all(v, axis, split_axis=0, concat_axis=0, tiled=True, axis_ind...  57.5 us
    all_to_all x4, starting transfers between devices, a2a(): lax.all_to_all(v, axis, split_axis=0, concat_axis=0, tiled=True, axis_ind...  29.1 us
    all_to_all x1, blocking collectives, a2a(): lax.all_to_all(v, axis, split_axis=0, concat_axis=0, tiled=True, axis_ind...  25.3 us
    pallas_call x1, Pallas kernels, hot_pool(): call(hot_kernel, (sds((BAGS, E), f32), sds((B, E), bf)), [VM] * 6, (), 2...  17.6 us
    pallas_call x1, Pallas kernels, hot_sum(): call(hot_grad_kernel, sds((HOT, E), f32), [VM] * 2, [pltpu.VMEM((BAGS, E)...  15.1 us
    pallas_call x1, Pallas kernels, cross(): call(kernel, (sds((B, 1), f32), sds((HB, 2 * E), bf)), [VM] * 7 + [ANY] *...  10.3 us
    pallas_call x1, Pallas kernels, slot_grads(): call(slot_kernel, sds((SLOTS, E), bf), [VM] * 2, (), 2 * BAGS * SLOTS * E...  5.2 us
    unnamed x24, local copies, waits for them, and re-layouts  4.87 us
  transfers between devices with their start and end apart: 6, of which 5 were waited for; matrix products, arithmetic and copies ran while one was open for 3% of the time, Pallas kernels for 14%

profile of v1, /device:TPU:8, one launch (start us, length us, event | category | flops | bytes accessed | tf_op | source)
XLA Modules:
  0.0 187.3 jit_solution(12013690676446549121)
XLA Ops:
  0.6 0.0 copy-start.4
  0.6 1.5 copy.32
  2.1 2.9 %shard_map.176 = bf16[3072,128]{1,0:T(8,128)(2,1)} custom-call(s32[1,12]{1,0:T(1,128)} %count_ref.3, s32[256,12]{1,0:T(8,128)} %bitcast.21, bf16[512,128]{1,0:T(8,128)(2,1)} %table_ref.5), custom_call_target="tpu_custom_call" | custom-call | flops 402653184 | bytes 2000000 | tf_op jit(solution)/shard_map/pallas_call | solution.py:211
  5.1 15.2 %all-to-all-start = ((bf16[12,256,128]{2,1,0:T(8,128)(2,1)}), bf16[12,256,128]{2,1,0:T(8,128)(2,1)S(1)}, u32[]{:S(2)}, u32[]{:S(2)}) async-start(bf16[12,256,128]{2,1,0:T(8,128)(2,1)} %bitcast.16), calls=%async_computation | async-start | bytes 1572864 | tf_op jit(solution)/shard_map/all_to_all | solution.py:258
  20.2 0.0 copy-done.4
  20.2 0.1 copy.30
  20.3 0.6 pad.4.ids_ref
  21.0 0.0 copy-done.7
  21.0 0.7 copy.31.dense_ref
  21.7 0.0 copy-done.5
  21.7 0.8 copy.33
  22.5 0.0 copy-done.9
  22.5 0.7 copy.34.refs_5_
  23.2 0.0 copy-done.6
  23.2 0.6 broadcast_in_dim.11.refs_6_
  23.8 17.6 %shard_map.175 = (f32[3328,128]{1,0:T(8,128)}, bf16[128,128]{1,0:T(8,128)(2,1)}) custom-call(s32[128,128]{1,0:T(8,128)} %pad.4.ids_ref, bf16[3072,128]{1,0:T(8,128)(2,1)} %table_ref.3, bf16[128,13]{1,0:T(8,128)(2,1)} %copy.31.dense_ref, bf16[13,512]{1,0:T(8,128)(2,1)} %one_ref.1, bf16[512,256]{1,0:T(8,128)(2,1)} %two_ref.1, bf16[256,128]{1,0:T(8,128)(2,1)} %three_ref.1), custom_call_target="tpu_custom_call" | custom-call | flops 2617245696 | bytes 4000000 | tf_op jit(solution)/shard_map/pallas_call | solution.py:217
  41.4 10.2 %all-to-all-done = bf16[12,256,128]{2,1,0:T(8,128)(2,1)S(1)} async-done(((bf16[12,256,128]{2,1,0:T(8,128)(2,1)}), bf16[12,256,128]{2,1,0:T(8,128)(2,1)S(1)}, u32[]{:S(2)}, u32[]{:S(2)}) %all-to-all-start) | async-done | bytes 786464 | tf_op jit(solution)/shard_map/all_to_all | solution.py:258
  51.6 0.9 copy-done
  52.5 10.3 %shard_map.177 = (f32[128,1]{1,0:T(8,128)}, bf16[1664,256]{1,0:T(8,128)(2,1)}) custom-call(f32[3328,128]{1,0:T(8,128)} %get-tuple-element.7.refs_0_, bf16[128,128]{1,0:T(8,128)(2,1)} %get-tuple-element.8.refs_1_, bf16[3072,128]{1,0:T(8,128)(2,1)} %bitcast.15, s32[12,256]{1,0:T(8,128)} %refs_3_.1, s32[256,12]{1,0:T(8,128)} %bitcast.19, ...), custom_call_target="tpu_custom_call" | custom-call | flops 4429185024 | bytes 12000000 | tf_op jit(solution)/shard_map/pallas_call | solution.py:226
  62.8 15.1 %shard_map.178 = f32[3072,128]{1,0:T(8,128)} custom-call(s32[52,128]{1,0:T(8,128)} %bitcast.22, bf16[1664,256]{1,0:T(8,128)(2,1)} %get-tuple-element.10.bag_grad_ref), custom_call_target="tpu_custom_call" | custom-call | flops 2617245696 | bytes 3000000 | tf_op jit(solution)/shard_map/pallas_call | solution.py:248
  77.9 1.2 dynamic-slice_convert_fusion
  79.0 1.9 %collective-permute-start = (bf16[1536,128]{1,0:T(8,128)(2,1)S(1)}, bf16[1536,128]{1,0:T(8,128)(2,1)S(1)}, u32[]{:S(2)}, u32[]{:S(2)}) collective-permute-start(bf16[1536,128]{1,0:T(8,128)(2,1)S(1)} %dynamic-slice_convert_fusion), channel_id=1, source_target_pairs={{0,12},{12,0},{24,36},{36,24},{48,60},{60,48},{72,84},{84,72},{96,... | collective-permute-start | bytes 1179656 | tf_op jit(solution)/shard_map/ppermute | solution.py:296
  81.0 1.7 collective-permute-done
  82.6 1.2 add_convert_fusion
  83.9 25.3 %all_to_all.46 = bf16[32,48,128]{2,1,0:T(8,128)(2,1)S(1)} all-to-all(bf16[32,48,128]{2,1,0:T(8,128)(2,1)S(1)} %bitcast.14), channel_id=1, replica_groups={{0,24,48,72,96,120,144,168,192,216,240,264,288,312,336,360,384,408,432,..., dimensions={0} | all-to-all | bytes 786432 | tf_op jit(solution)/shard_map/all_to_all | solution.py:258
  109.1 0.1 reduce_sum.30
  109.2 0.7 broadcast_in_dim.24
  109.9 4.4 %all-to-all-start.2 = ((bf16[12,48,128]{2,1,0:T(8,128)(2,1)}), bf16[12,48,128]{2,1,0:T(8,128)(2,1)S(1)}, u32[]{:S(2)}, u32[]{:S(2)}) async-start(bf16[12,48,128]{2,1,0:T(8,128)(2,1)} %broadcast_in_dim.24), calls=%async_computation.2 | async-start | bytes 294912 | tf_op jit(solution)/shard_map/all_to_all | solution.py:258
  114.4 11.9 %all-to-all-done.2 = bf16[12,48,128]{2,1,0:T(8,128)(2,1)S(1)} async-done(((bf16[12,48,128]{2,1,0:T(8,128)(2,1)}), bf16[12,48,128]{2,1,0:T(8,128)(2,1)S(1)}, u32[]{:S(2)}, u32[]{:S(2)}) %all-to-all-start.2) | async-done | bytes 147488 | tf_op jit(solution)/shard_map/all_to_all | solution.py:258
  126.3 0.1 multiply_reduce_fusion
  126.4 0.8 add_sqrt_fusion
  127.1 0.1 divide_convert_fusion
  127.2 0.8 broadcast_in_dim.25
  128.0 5.3 %all-to-all-start.3 = ((bf16[32,48,128]{2,1,0:T(8,128)(2,1)}), bf16[32,48,128]{2,1,0:T(8,128)(2,1)S(1)}, u32[]{:S(2)}, u32[]{:S(2)}) async-start(bf16[32,48,128]{2,1,0:T(8,128)(2,1)} %broadcast_in_dim.25), calls=%async_computation.3 | async-start | bytes 786432 | tf_op jit(solution)/shard_map/all_to_all | solution.py:258
  133.3 5.2 %shard_map.179 = bf16[3072,128]{1,0:T(8,128)(2,1)} custom-call(s32[256,12]{1,0:T(8,128)} %bitcast.20, bf16[1664,256]{1,0:T(8,128)(2,1)} %get-tuple-element.10.bag_grad_ref), custom_call_target="tpu_custom_call" | custom-call | flops 2617245696 | bytes 2000000 | tf_op jit(solution)/shard_map/pallas_call | solution.py:244
  138.5 7.8 %all-to-all-done.3 = bf16[32,48,128]{2,1,0:T(8,128)(2,1)S(1)} async-done(((bf16[32,48,128]{2,1,0:T(8,128)(2,1)}), bf16[32,48,128]{2,1,0:T(8,128)(2,1)S(1)}, u32[]{:S(2)}, u32[]{:S(2)}) %all-to-all-start.3) | async-done | bytes 393248 | tf_op jit(solution)/shard_map/all_to_all | solution.py:258
  146.3 4.2 %all-to-all-start.4 = ((bf16[12,256,128]{2,1,0:T(8,128)(2,1)}), bf16[12,256,128]{2,1,0:T(8,128)(2,1)S(1)}, u32[]{:S(2)}, u32[]{:S(2)}) async-start(bf16[12,256,128]{2,1,0:T(8,128)(2,1)} %bitcast.17), calls=%async_computation.4 | async-start | bytes 1572864 | tf_op jit(solution)/shard_map/all_to_all | solution.py:258
  150.5 1.9 %collective-permute-start.1 = (bf16[1536,128]{1,0:T(8,128)(2,1)S(1)}, bf16[1536,128]{1,0:T(8,128)(2,1)S(1)}, u32[]{:S(2)}, u32[]{:S(2)}) collective-permute-start(bf16[1536,128]{1,0:T(8,128)(2,1)S(1)} %bitcast.13), channel_id=1, source_target_pairs={{0,12},{12,0},{24,36},{36,24},{48,60},{60,48},{72,84},{84,72},{96,... | collective-permute-start | bytes 1179656 | tf_op jit(solution)/shard_map/ppermute | solution.py:310
  152.5 0.0 copy-done.8
  152.5 0.9 copy.35.accum_ref
  153.3 0.0 copy-done.3
  153.3 0.6 reduce.2
  154.0 27.7 %all-to-all-done.4 = bf16[12,256,128]{2,1,0:T(8,128)(2,1)S(1)} async-done(((bf16[12,256,128]{2,1,0:T(8,128)(2,1)}), bf16[12,256,128]{2,1,0:T(8,128)(2,1)S(1)}, u32[]{:S(2)}, u32[]{:S(2)}) %all-to-all-start.4) | async-done | bytes 786464 | tf_op jit(solution)/shard_map/all_to_all | solution.py:258
  181.7 0.9 copy-done.1
  182.5 3.4 %shard_map.180 = f32[512,128]{1,0:T(8,128)} custom-call(s32[1,12]{1,0:T(1,128)} %count_ref.3, s32[12,256]{1,0:T(8,128)} %rows_ref.1, bf16[3072,128]{1,0:T(8,128)(2,1)} %bitcast.18, bf16[512,128]{1,0:T(8,128)(2,1)} %table_ref.5, f32[512,1]{1,0:T(8,128)} %copy.35.accum_ref), custom_call_target="tpu_custom_call" | custom-call | flops 402653184 | bytes 2000000 | tf_op jit(solution)/shard_map/pallas_call | solution.py:252
  185.9 0.0 collective-permute-done.1
  185.9 0.1 broadcast_select_fusion.1
  186.0 1.3 convert_subtract_fusion
  (11 shorter events, 0.0 us)
Async XLA Ops:
  0.6 19.6 %copy-start.4 = (s32[128,52]{0,1:T(8,128)S(1)}, s32[128,52]{0,1:T(8,128)}, u32[]{:S(2)}) copy-start(s32[128,52]{0,1:T(8,128)} %param.17) | copy-start | bytes 79876
  2.1 18.8 %copy-start.7 = (bf16[128,13]{0,1:T(8,128)(2,1)S(1)}, bf16[128,13]{0,1:T(8,128)(2,1)}, u32[]{:S(2)}) copy-start(bf16[128,13]{0,1:T(8,128)(2,1)} %param.16) | copy-start | bytes 9988
  2.1 19.6 %copy-start.5 = (s32[12,256]{1,0:T(8,128)S(1)}, s32[12,256]{1,0:T(8,128)}, u32[]{:S(2)}) copy-start(s32[12,256]{1,0:T(8,128)} %refs_3_.1) | copy-start | bytes 36868
  2.1 20.3 %copy-start.9 = (f32[128]{0:T(128)S(1)}, f32[128]{0:T(128)}, u32[]{:S(2)}) copy-start(f32[128]{0:T(128)} %param.18) | copy-start | bytes 1540
  2.1 21.1 %copy-start.6 = (f32[3456]{0:T(1024)S(1)}, f32[3456]{0:T(1024)}, u32[]{:S(2)}) copy-start(f32[3456]{0:T(1024)} %param.31) | copy-start | bytes 41476
  5.1 46.5 %all-to-all-start = ((bf16[12,256,128]{2,1,0:T(8,128)(2,1)}), bf16[12,256,128]{2,1,0:T(8,128)(2,1)S(1)}, u32[]{:S(2)}, u32[]{:S(2)}) async-start(bf16[12,256,128]{2,1,0:T(8,128)(2,1)} %bitcast.16), calls=%async_computation | async-start | bytes 1572864 | tf_op jit(solution)/shard_map/all_to_all | solution.py:258
  51.6 0.9 copy-start
  79.0 3.6 %collective-permute-start = (bf16[1536,128]{1,0:T(8,128)(2,1)S(1)}, bf16[1536,128]{1,0:T(8,128)(2,1)S(1)}, u32[]{:S(2)}, u32[]{:S(2)}) collective-permute-start(bf16[1536,128]{1,0:T(8,128)(2,1)S(1)} %dynamic-slice_convert_fusion), channel_id=1, source_target_pairs={{0,12},{12,0},{24,36},{36,24},{48,60},{60,48},{72,84},{84,72},{96,... | collective-permute-start | bytes 1179656 | tf_op jit(solution)/shard_map/ppermute | solution.py:296
  109.9 16.3 %all-to-all-start.2 = ((bf16[12,48,128]{2,1,0:T(8,128)(2,1)}), bf16[12,48,128]{2,1,0:T(8,128)(2,1)S(1)}, u32[]{:S(2)}, u32[]{:S(2)}) async-start(bf16[12,48,128]{2,1,0:T(8,128)(2,1)} %broadcast_in_dim.24), calls=%async_computation.2 | async-start | bytes 294912 | tf_op jit(solution)/shard_map/all_to_all | solution.py:258
  128.0 18.3 %all-to-all-start.3 = ((bf16[32,48,128]{2,1,0:T(8,128)(2,1)}), bf16[32,48,128]{2,1,0:T(8,128)(2,1)S(1)}, u32[]{:S(2)}, u32[]{:S(2)}) async-start(bf16[32,48,128]{2,1,0:T(8,128)(2,1)} %broadcast_in_dim.25), calls=%async_computation.3 | async-start | bytes 786432 | tf_op jit(solution)/shard_map/all_to_all | solution.py:258
  138.5 13.9 %copy-start.8 = (f32[512]{0:T(512)S(1)}, f32[512]{0:T(512)}, u32[]{:S(2)}) copy-start(f32[512]{0:T(512)} %param.22) | copy-start | bytes 6148
  138.5 14.8 %copy-start.3 = (f32[128,1]{1,0:T(8,128)S(1)}, f32[128,1]{1,0:T(8,128)}, u32[]{:S(2)}) copy-start(f32[128,1]{1,0:T(8,128)} %get-tuple-element.9) | copy-start | bytes 1540
  146.3 35.4 %all-to-all-start.4 = ((bf16[12,256,128]{2,1,0:T(8,128)(2,1)}), bf16[12,256,128]{2,1,0:T(8,128)(2,1)S(1)}, u32[]{:S(2)}, u32[]{:S(2)}) async-start(bf16[12,256,128]{2,1,0:T(8,128)(2,1)} %bitcast.17), calls=%async_computation.4 | async-start | bytes 1572864 | tf_op jit(solution)/shard_map/all_to_all | solution.py:258
  150.5 35.4 %collective-permute-start.1 = (bf16[1536,128]{1,0:T(8,128)(2,1)S(1)}, bf16[1536,128]{1,0:T(8,128)(2,1)S(1)}, u32[]{:S(2)}, u32[]{:S(2)}) collective-permute-start(bf16[1536,128]{1,0:T(8,128)(2,1)S(1)} %bitcast.13), channel_id=1, source_target_pairs={{0,12},{12,0},{24,36},{36,24},{48,60},{60,48},{72,84},{84,72},{96,... | collective-permute-start | bytes 1179656 | tf_op jit(solution)/shard_map/ppermute | solution.py:310
  153.3 32.7 %copy-start.2 = (bf16[3072,128]{1,0:T(8,128)(2,1)S(1)}, bf16[3072,128]{1,0:T(8,128)(2,1)}, u32[]{:S(2)}) copy-start(bf16[3072,128]{1,0:T(8,128)(2,1)} %table_ref.3) | copy-start | bytes 2359300
  181.6 0.9 copy-start.1

commit v2 on v1

v2 whole, which is shorter than its diff:
```python
import jax
import jax.numpy as jnp
from jax import lax
from jax.experimental import pallas as pl
from jax.experimental.pallas import tpu as pltpu
from jax.sharding import PartitionSpec as P

E = 128
TABLES = 26
HALF = 13
LH = 2
HOT = 3072
B = 128
ROWS = 512
CAP = 256
NT = 12
SLOTS = NT * CAP
BAGS = B * TABLES
HB = B * HALF
R = 512
F = 3456
f32 = jnp.float32
bf = jnp.bfloat16
MIB = 1024 * 1024
VM = pl.BlockSpec(memory_space=pltpu.VMEM)
ANY = pl.BlockSpec(memory_space=pl.ANY)
SM = pl.BlockSpec(memory_space=pltpu.SMEM)


def dot(a, b):
    return jnp.dot(a, b, preferred_element_type=f32)


def dot_t(a, b):
    return lax.dot_general(a, b, (((1,), (1,)), ((), ())), preferred_element_type=f32)


def hit(idx, base, shape, axis):
    place = lax.broadcasted_iota(jnp.int32, shape, axis)
    return jnp.where(idx - base == place, 1.0, 0.0).astype(bf)


def call(kernel, outs, n_in_specs, scratch=(), flops=0, nbytes=0, mib=24):
    return pl.pallas_call(
        kernel,
        out_shape=outs,
        in_specs=n_in_specs,
        out_specs=jax.tree.map(lambda _: VM, outs),
        scratch_shapes=list(scratch),
        compiler_params=pltpu.CompilerParams(vmem_limit_bytes=mib * MIB),
        cost_estimate=pl.CostEstimate(flops=flops, bytes_accessed=nbytes, transcendentals=0),
    )


def split_bag(bag):
    sample = (bag * 2521) >> 16
    table = bag - sample * TABLES
    upper = table >= HALF
    return upper, jnp.where(upper, table - HALF, table) * B + sample


def pick_kernel(count_ref, rows_ref, table_ref, out_ref, wide):
    rows_t = rows_ref[...].T
    wide[:, :E] = table_ref[: ROWS // 2, :]
    wide[:, E:] = table_ref[ROWS // 2 :, :]
    slot = lax.broadcasted_iota(jnp.int32, (CAP, 1), 0)
    for s in range(NT):
        row = rows_t[:, s : s + 1]
        row = jnp.where(slot < count_ref[0, s], row, -1)
        upper = row >= ROWS // 2
        low = jnp.where(upper, row - ROWS // 2, row)
        both = dot(hit(low, 0, (CAP, ROWS // 2), 1), wide[...])
        out_ref[s * CAP : (s + 1) * CAP, :] = jnp.where(upper, both[:, E:], both[:, :E]).astype(bf)


def hot_kernel(ids_ref, table_ref, dense_ref, one_ref, two_ref, three_ref, out_ref, bottom_ref):
    first = jnp.maximum(dot(dense_ref[...], one_ref[...]), 0.0).astype(bf)
    second = jnp.maximum(dot(first, two_ref[...]), 0.0).astype(bf)
    bottom_ref[...] = jnp.maximum(dot(second, three_ref[...]), 0.0).astype(bf)

    def pair(j, _):
        ids = pltpu.roll(ids_ref[...], lax.rem(128 - 4 * j, 128), 1)
        left = jnp.concatenate([ids[:, 0:1], ids[:, 2:3]], axis=0)
        right = jnp.concatenate([ids[:, 1:2], ids[:, 3:4]], axis=0)
        count = hit(left, 0, (2 * B, HOT), 1) + hit(right, 0, (2 * B, HOT), 1)
        out_ref[pl.ds(pl.multiple_of(j * 2 * B, 2 * B), 2 * B), :] = dot(count, table_ref[...])
        return 0

    lax.fori_loop(0, HALF, pair, 0)


HK = 4
HQ = HOT // HK
HT = 26
SG = 4


def mark(idx, shape, axis):
    place = lax.broadcasted_iota(jnp.int16, shape, axis)
    return jnp.where(idx.astype(jnp.int16) == place, jnp.ones(shape, bf), jnp.zeros(shape, bf))


def spot(t):
    r = (t % HALF) * B
    c = (t // HALF) * E
    return slice(r, r + B), slice(c, c + E)


def cross_kernel(
    hot_ref,
    bottom_ref,
    arrived_ref,
    bags_ref,
    bags_t_ref,
    grad_ref,
    head_ref,
    down_hbm,
    up_hbm,
    logits_ref,
    bag_grad_ref,
    slot_ref,
    down,
    up,
    cold,
    x0,
    sems,
):
    copy_down = pltpu.make_async_copy(down_hbm, down, sems.at[0])
    copy_up = pltpu.make_async_copy(up_hbm, up, sems.at[1])
    copy_down.start()
    copy_up.start()
    zero = jnp.zeros((CAP, E), bf)
    _, place = split_bag(bags_ref[...])
    for g in range(2):
        owners = range(6 * g, 6 * g + 6)
        wide = []
        for s in owners:
            upper, _ = split_bag(bags_t_ref[:, s : s + 1])
            block = arrived_ref[s * CAP : (s + 1) * CAP, :]
            wide.append(jnp.concatenate([jnp.where(upper, zero, block), jnp.where(upper, block, zero)], axis=1))
        flat = jnp.concatenate([place[s : s + 1, :] for s in owners], axis=1)
        part = dot(mark(flat, (HB, 6 * CAP), 0), jnp.concatenate(wide, axis=0))
        cold[...] = part if g == 0 else cold[...] + part
    x0[:, :E] = bottom_ref[...]
    for t in range(TABLES):
        r, c = spot(t)
        x0[:, E * (t + 1) : E * (t + 2)] = (hot_ref[t * B : (t + 1) * B, :] + cold[r, c]).astype(bf)
    upstream = grad_ref[...]
    copy_down.wait()
    copy_up.wait()
    low = dot(x0[...], down[...]).astype(bf)
    low_grad = dot_t((upstream * head_ref[...] * x0[...].astype(f32)).astype(bf), up[...]).astype(bf)
    logit = jnp.zeros((B, E), f32)
    for k in range(0, TABLES + 1, 3):
        cols = slice(E * k, E * (k + 3))
        head = head_ref[:, cols]
        gated = dot(low, up[:, cols]) + 1.0
        part = x0[:, cols].astype(f32) * gated * head
        logit = logit + part[:, :E] + part[:, E : 2 * E] + part[:, 2 * E :]
        back = upstream * head * gated + dot_t(low_grad, down[cols, :])
        for i in range(3):
            if k + i > 0:
                r, c = spot(k + i - 1)
                bag_grad_ref[r, c] = back[:, E * i : E * (i + 1)].astype(bf)
    logits_ref[...] = jnp.sum(logit, axis=1, keepdims=True)
    for g in range(0, NT, SG):
        halves, marks = [], []
        for s in range(g, g + SG):
            upper, place = split_bag(bags_t_ref[:, s : s + 1])
            halves.append(upper)
            marks.append(hit(place, 0, (CAP, HB), 1))
        both = dot(jnp.concatenate(marks, axis=0), bag_grad_ref[...])
        upper = jnp.concatenate(halves, axis=0)
        slot_ref[g * CAP : (g + SG) * CAP, :] = jnp.where(upper, both[:, E:], both[:, :E]).astype(bf)


def hot_grad_kernel(core_ref, bag_grad_ref, ids_ref, ids_t_ref, mine_ref, other_ref, total):
    none = jnp.zeros((B, E), bf)
    low_ids = lax.rem(ids_t_ref[...], HQ)
    for g in range(TABLES * LH // HT):
        places, blocks = [], []
        for i in range(HT):
            n = g * HT + i
            r, c = spot(n // LH)
            block = bag_grad_ref[r, c]
            col = ids_ref[:, n : n + 1]
            blocks.append(
                jnp.concatenate(
                    [jnp.where((col >= q * HQ) & (col < (q + 1) * HQ), block, none) for q in range(HK)], axis=1
                )
            )
            places.append(low_ids[n : n + 1, :])
        part = dot(
            mark(jnp.concatenate(places, axis=1), (HQ, HT * B), 0), jnp.concatenate(blocks, axis=0)
        )
        total[...] = part if g == 0 else total[...] + part
    first = core_ref[0] == 0
    for q in range(HK // 2):
        lower = total[:, q * E : (q + 1) * E]
        higher = total[:, (q + HK // 2) * E : (q + HK // 2 + 1) * E]
        rows = slice(q * HQ, (q + 1) * HQ)
        mine_ref[rows, :] = jnp.where(first, lower, higher)
        other_ref[rows, :] = jnp.where(first, higher, lower).astype(bf)


def share_kernel(x_ref, mine_ref, met_ref, own_ref, one_ref, two_ref, three_ref):
    part = own_ref.shape[0]
    for k, out in enumerate((own_ref, one_ref, two_ref, three_ref)):
        start = pl.multiple_of(lax.rem(x_ref[0] + k, 4) * part, part)
        chip = mine_ref[pl.ds(start, part), :] + met_ref[pl.ds(start, part), :].astype(f32)
        out[...] = chip.astype(out.dtype)


def cold_kernel(count_ref, rows_ref, returned_ref, table_ref, accum_ref, out_ref):
    lane = lax.broadcasted_iota(jnp.int32, (1, CAP), 1)
    flat = jnp.concatenate(
        [jnp.where(lane < count_ref[0, s], rows_ref[s : s + 1, :], -1) for s in range(NT)], axis=1
    )
    grad = dot(hit(flat, 0, (ROWS, SLOTS), 0), returned_ref[...])
    updated = accum_ref[...] + jnp.mean(grad * grad, axis=1, keepdims=True)
    out_ref[...] = table_ref[...].astype(f32) - grad / jnp.sqrt(updated)


def sds(shape, dtype):
    return jax.ShapeDtypeStruct(shape, dtype)


def pick(count, rows_t, table):
    return call(pick_kernel, sds((SLOTS, E), bf), [SM, VM, VM], [pltpu.VMEM((ROWS // 2, 2 * E), bf)], 2 * SLOTS * ROWS * E, 2000000)(
        count, rows_t, table
    )


def hot_pool(ids, table, dense, one, two, three):
    return call(hot_kernel, (sds((BAGS, E), f32), sds((B, E), bf)), [VM] * 6, (), 2 * BAGS * HOT * E, 4000000)(
        ids, table, dense, one, two, three
    )


def cross(hot, bottom, arrived, bags, bags_t, grad, head, down, up):
    return call(
        cross_kernel,
        (sds((B, 1), f32), sds((HB, 2 * E), bf), sds((SLOTS, E), bf)),
        [VM] * 7 + [ANY] * 2,
        [
            pltpu.VMEM((F, R), bf),
            pltpu.VMEM((R, F), bf),
            pltpu.VMEM((HB, 2 * E), f32),
            pltpu.VMEM((B, F), bf),
            pltpu.SemaphoreType.DMA((2,)),
        ],
        4 * BAGS * SLOTS * E + 8 * B * F * R,
        14000000,
        60,
    )(hot, bottom, arrived, bags, bags_t, grad, head, down, up)


def hot_sum(core, bag_grad, ids, ids_t):
    return call(
        hot_grad_kernel,
        (sds((HOT // 2, E), f32), sds((HOT // 2, E), bf)),
        [SM] + [VM] * 3,
        [pltpu.VMEM((HQ, HK * E), f32)],
        2 * BAGS * HOT * E,
        3000000,
        32,
    )(core, bag_grad, ids, ids_t)


def shares(x, mine, met):
    part = HOT // 8
    return call(
        share_kernel,
        (sds((part, E), f32),) + (sds((part, E), bf),) * 3,
        [SM] + [VM] * 2,
        (),
        HOT * E,
        2000000,
    )(x, mine, met)


def cold_update(count, rows, returned, table, accum):
    return call(cold_kernel, sds((ROWS, E), f32), [SM] + [VM] * 4, (), 2 * ROWS * SLOTS * E, 2000000)(
        count, rows, returned, table, accum
    )


def a2a(v, axis, groups=None):
    return lax.all_to_all(v, axis, split_axis=0, concat_axis=0, tiled=True, axis_index_groups=groups)


def body(
    dense_input,
    hot_ids,
    logit_grad,
    hot_table,
    hot_accum,
    cold_table,
    cold_accum,
    send_rows,
    send_count,
    recv_bags,
    bottom_one,
    bottom_two,
    bottom_three,
    cross_down,
    cross_up,
    head_vector,
):
    n_dp = lax.axis_size("dp")
    n_xy = n_dp // 2
    n_y = n_xy // 4
    xy_groups = [[2 * k + c for k in range(n_xy)] for c in range(2)]
    y_groups = [[2 * n_y * x + 2 * y + c for y in range(n_y)] for x in range(4) for c in range(2)]
    twin = [(i, i ^ 1) for i in range(n_dp)]
    outgoing = pick(send_count, send_rows, cold_table)
    arrived = a2a(outgoing, "table")
    bags_t = recv_bags.T
    ids = jnp.pad(hot_ids, ((0, 0), (0, 128 - TABLES * LH)))
    hot, bottom = hot_pool(ids, hot_table, dense_input, bottom_one, bottom_two, bottom_three)
    core = lax.rem(lax.axis_index("dp"), 2)
    x_at = lax.div(lax.axis_index("dp"), 2 * n_y)
    half = HOT // 2
    logits, bag_grad, slot_grad = cross(
        hot, bottom, arrived, recv_bags, bags_t, logit_grad[:, None], head_vector[None, :], cross_down, cross_up
    )
    returned = a2a(slot_grad, "table")
    mine, other = hot_sum(core[None], bag_grad, hot_ids, hot_ids.T)
    met = lax.ppermute(other, "dp", twin)
    total, *parts = shares(x_at[None], mine, met)
    for k in range(1, 4):
        ahead = [(i, (i + 2 * n_y * k) % n_dp) for i in range(n_dp)]
        total = total + lax.ppermute(parts[k - 1], "dp", ahead).astype(f32)
    total, returned = lax.optimization_barrier((total.astype(bf), returned))
    share = half // n_xy
    line = a2a(total, "dp", y_groups)
    plane = jnp.sum(line.reshape(n_y, share, E).astype(f32), axis=0).astype(bf)
    column = a2a(jnp.broadcast_to(plane[None], (NT, share, E)).reshape(NT * share, E), "table")
    grad = jnp.sum(column.reshape(NT, share, E).astype(f32), axis=0)
    first = core * half + lax.div(lax.axis_index("dp"), 2) * share
    accum = lax.dynamic_slice_in_dim(hot_accum, first, share, 0)
    step = grad / jnp.sqrt(accum + jnp.mean(grad * grad, axis=1))[:, None]
    step = step.astype(bf)
    steps = a2a(jnp.broadcast_to(step[None], (n_xy, share, E)).reshape(half, E), "dp", xy_groups)
    others = lax.ppermute(steps, "dp", twin)
    low = jnp.where(core == 0, steps, others)
    high = jnp.where(core == 0, others, steps)
    new_hot = hot_table.astype(f32) - jnp.concatenate([low, high], axis=0).astype(f32)
    new_cold = cold_update(send_count, send_rows, returned, cold_table, cold_accum[:, None])
    return (logits[:, 0], new_hot, new_cold)


def solution(mesh):
    rows = P(("dp", "table"), None)
    flat = P(("dp", "table"))
    return jax.shard_map(
        body,
        mesh=mesh,
        in_specs=(rows, rows, flat, P(), P(), rows, flat, rows, rows, rows, P(), P(), P(), P(), P(), P()),
        out_specs=(flat, P(), rows),
        check_vma=False,
    )
```

time: 188 us -> 165 us (0.88)
  the two profiles are of different devices: /device:TPU:8 before, /device:TPU:1 now
where the time goes in v2:
time: 165 us
  starting transfers between devices  51.9 us (31%)
  Pallas kernels  42.5 us (26%)
  blocking collectives  29 us (18%)
  waiting for transfers between devices  27.7 us (17%)
  local copies, waits for them, and re-layouts  9.51 us (6%)
  other arithmetic  3.08 us (2%)
    all_to_all x3, starting transfers between devices, a2a(): lax.all_to_all(v, axis, split_axis=0, concat_axis=0, tiled=True, axis_ind...  31 us
    all_to_all x2, blocking collectives, a2a(): lax.all_to_all(v, axis, split_axis=0, concat_axis=0, tiled=True, axis_ind...  29 us
    all_to_all x3, waiting for transfers between devices, a2a(): lax.all_to_all(v, axis, split_axis=0, concat_axis=0, tiled=True, axis_ind...  22.2 us
    pallas_call x1, Pallas kernels, cross(): call(cross_kernel, (sds((B, 1), f32), sds((HB, 2 * E), bf), sds((SLOTS, E...  16.3 us
    pallas_call x1, Pallas kernels, hot_pool(): call(hot_kernel, (sds((BAGS, E), f32), sds((B, E), bf)), [VM] * 6, (), 2...  15.2 us
    ppermute x3, starting transfers between devices, body(): total = total + lax.ppermute(parts[k - 1], 'dp', ahead).astype(f32)  9.46 us
    ppermute x1, starting transfers between devices, body(): others = lax.ppermute(steps, 'dp', twin)  8.47 us
    unnamed x45, local copies, waits for them, and re-layouts  7.29 us
  transfers between devices with their start and end apart: 8, of which 6 were waited for; matrix products, arithmetic and copies ran while one was open for 2% of the time, Pallas kernels for 14%

profile of v2, /device:TPU:1, one launch (start us, length us, event | category | flops | bytes accessed | tf_op | source)
XLA Modules:
  0.0 164.7 jit_solution(12136808335152029866)
XLA Ops:
  0.7 0.0 copy-start.3
  0.7 1.0 copy-done.3
  1.7 0.7 copy-done.7
  2.4 0.7 copy-done.9
  3.1 2.5 %shard_map.176 = bf16[3072,128]{1,0:T(8,128)(2,1)} custom-call(s32[1,12]{1,0:T(1,128)S(1)} %copy-done.9, s32[12,256]{1,0:T(8,128)S(1)} %copy-done.7, bf16[512,128]{1,0:T(8,128)(2,1)S(1)} %copy-done.3), custom_call_target="tpu_custom_call" | custom-call | flops 402653184 | bytes 2000000 | tf_op jit(solution)/shard_map/pallas_call | solution.py:229
  5.6 15.7 %all-to-all-start = ((bf16[12,256,128]{2,1,0:T(8,128)(2,1)}), bf16[12,256,128]{2,1,0:T(8,128)(2,1)S(1)}, u32[]{:S(2)}, u32[]{:S(2)}) async-start(bf16[12,256,128]{2,1,0:T(8,128)(2,1)} %bitcast), calls=%async_computation | async-start | bytes 1572864 | tf_op jit(solution)/shard_map/all_to_all | solution.py:289
  21.3 0.1 copy.30.ids_ref
  21.4 0.1 copy.31.dense_ref
  21.5 0.8 copy.32
  22.3 0.7 copy.33.grad_ref
  23.0 0.6 broadcast_in_dim.29.head_ref
  23.7 15.2 %shard_map.175 = (f32[3328,128]{1,0:T(8,128)S(1)}, bf16[128,128]{1,0:T(8,128)(2,1)S(1)}) custom-call(s32[128,128]{1,0:T(8,128)S(1)} %pad.4.ids_ref, bf16[3072,128]{1,0:T(8,128)(2,1)S(1)} %copy-done, bf16[128,13]{1,0:T(8,128)(2,1)S(1)} %copy.31.dense_ref, bf16[13,512]{1,0:T(8,128)(2,1)S(1)} %copy-done.6, bf16[512,256]{1,0:T(8,128)(2,1)S(1)} %copy-done.2, ...), custom_call_target="tpu_custom_call" | custom-call | flops 2617245696 | bytes 4000000 | tf_op jit(solution)/shard_map/pallas_call | solution.py:235
  38.9 1.2 copy-done.11
  40.2 0.6 copy-done.13
  40.8 8.6 %all-to-all-done = bf16[12,256,128]{2,1,0:T(8,128)(2,1)S(1)} async-done(((bf16[12,256,128]{2,1,0:T(8,128)(2,1)}), bf16[12,256,128]{2,1,0:T(8,128)(2,1)S(1)}, u32[]{:S(2)}, u32[]{:S(2)}) %all-to-all-start) | async-done | bytes 786464 | tf_op jit(solution)/shard_map/all_to_all | solution.py:289
  49.4 0.9 copy-done.14
  50.3 16.3 %shard_map.177 = (f32[128,1]{1,0:T(8,128)}, bf16[1664,256]{1,0:T(8,128)(2,1)}, bf16[3072,128]{1,0:T(8,128)(2,1)}) custom-call(f32[3328,128]{1,0:T(8,128)} %copy-done.11, bf16[128,128]{1,0:T(8,128)(2,1)} %copy-done.13, bf16[3072,128]{1,0:T(8,128)(2,1)} %bitcast.18, s32[12,256]{1,0:T(8,128)} %bags_ref.1, s32[256,12]{1,0:T(8,128)} %bitcast.20, ...), custom_call_target="tpu_custom_call" | custom-call | flops 7046430720 | bytes 14000000 | tf_op jit(solution)/shard_map/pallas_call | solution.py:241
  66.6 7.6 %all-to-all-start.1 = ((bf16[12,256,128]{2,1,0:T(8,128)(2,1)}), bf16[12,256,128]{2,1,0:T(8,128)(2,1)S(1)}, u32[]{:S(2)}, u32[]{:S(2)}) async-start(bf16[12,256,128]{2,1,0:T(8,128)(2,1)} %bitcast.17), calls=%async_computation.1 | async-start | bytes 1572864 | tf_op jit(solution)/shard_map/all_to_all | solution.py:289
  74.2 0.0 copy-start.12
  74.2 1.1 copy-done.12
  75.4 5.7 %shard_map.178 = (f32[1536,128]{1,0:T(8,128)S(1)}, bf16[1536,128]{1,0:T(8,128)(2,1)S(1)}) custom-call(s32[1]{0:T(128)} %bitcast.5.core_ref, bf16[1664,256]{1,0:T(8,128)(2,1)S(1)} %copy-done.12, s32[128,52]{1,0:T(8,128)S(1)} %copy.30.ids_ref, s32[52,128]{1,0:T(8,128)S(1)} %bitcast.15), custom_call_target="tpu_custom_call" | custom-call | flops 2617245696 | bytes 3000000 | tf_op jit(solution)/shard_map/pallas_call | solution.py:259
  81.1 3.0 %collective-permute-start = (bf16[1536,128]{1,0:T(8,128)(2,1)S(1)}, bf16[1536,128]{1,0:T(8,128)(2,1)S(1)}, u32[]{:S(2)}, u32[]{:S(2)}) collective-permute-start(bf16[1536,128]{1,0:T(8,128)(2,1)S(1)} %get-tuple-element.21), channel_id=1, source_target_pairs={{0,12},{12,0},{24,36},{36,24},{48,60},{60,48},{72,84},{84,72},{96,... | collective-permute-start | bytes 1179656 | tf_op jit(solution)/shard_map/ppermute | solution.py:329
  84.1 1.3 collective-permute-done.met_ref
  85.4 0.1 shard_map.179
  85.5 0.0 copy-start.19
  85.5 0.0 copy-start.10
  85.5 4.5 %collective-permute-start.3 = (bf16[384,128]{1,0:T(8,128)(2,1)S(1)}, bf16[384,128]{1,0:T(8,128)(2,1)S(1)}, u32[]{:S(2)}, u32[]{:S(2)}) collective-permute-start(bf16[384,128]{1,0:T(8,128)(2,1)S(1)} %get-tuple-element.25), channel_id=1, source_target_pairs={{0,576},{12,588},{24,600},{36,612},{48,624},{60,636},{72,648},{84,... | collective-permute-start | bytes 294920 | tf_op jit(solution)/shard_map/ppermute | solution.py:333
  90.1 2.4 %collective-permute-start.2 = (bf16[384,128]{1,0:T(8,128)(2,1)S(1)}, bf16[384,128]{1,0:T(8,128)(2,1)S(1)}, u32[]{:S(2)}, u32[]{:S(2)}) collective-permute-start(bf16[384,128]{1,0:T(8,128)(2,1)S(1)} %get-tuple-element.24), channel_id=1, source_target_pairs={{0,384},{12,396},{24,408},{36,420},{48,432},{60,444},{72,456},{84,... | collective-permute-start | bytes 294920 | tf_op jit(solution)/shard_map/ppermute | solution.py:333
  92.5 2.5 %collective-permute-start.1 = (bf16[384,128]{1,0:T(8,128)(2,1)S(1)}, bf16[384,128]{1,0:T(8,128)(2,1)S(1)}, u32[]{:S(2)}, u32[]{:S(2)}) collective-permute-start(bf16[384,128]{1,0:T(8,128)(2,1)S(1)} %get-tuple-element.23), channel_id=1, source_target_pairs={{0,192},{12,204},{24,216},{36,228},{48,240},{60,252},{72,264},{84,... | collective-permute-start | bytes 294920 | tf_op jit(solution)/shard_map/ppermute | solution.py:333
  95.0 1.9 %collective-permute-done.2 = bf16[384,128]{1,0:T(8,128)(2,1)S(1)} collective-permute-done((bf16[384,128]{1,0:T(8,128)(2,1)S(1)}, bf16[384,128]{1,0:T(8,128)(2,1)S(1)}, u32[]{:S(2)}, u32[]{:S(2)}) %collective-permute-start.2) | collective-permute-done | bytes 98336 | tf_op jit(solution)/shard_map/ppermute | solution.py:333
  96.9 2.3 %collective-permute-done.1 = bf16[384,128]{1,0:T(8,128)(2,1)S(1)} collective-permute-done((bf16[384,128]{1,0:T(8,128)(2,1)S(1)}, bf16[384,128]{1,0:T(8,128)(2,1)S(1)}, u32[]{:S(2)}, u32[]{:S(2)}) %collective-permute-start.1) | collective-permute-done | bytes 98336 | tf_op jit(solution)/shard_map/ppermute | solution.py:333
  99.2 0.1 add_convert_fusion
  99.3 2.8 %all-to-all-done.1 = bf16[12,256,128]{2,1,0:T(8,128)(2,1)S(1)} async-done(((bf16[12,256,128]{2,1,0:T(8,128)(2,1)}), bf16[12,256,128]{2,1,0:T(8,128)(2,1)S(1)}, u32[]{:S(2)}, u32[]{:S(2)}) %all-to-all-start.1) | async-done | bytes 786464 | tf_op jit(solution)/shard_map/all_to_all | solution.py:289
  102.1 14.2 %all_to_all.47 = bf16[8,48,128]{2,1,0:T(8,128)(2,1)S(1)} all-to-all(bf16[8,48,128]{2,1,0:T(8,128)(2,1)S(1)} %bitcast.19), channel_id=1, replica_groups={{0,24,48,72,96,120,144,168},{12,36,60,84,108,132,156,180},{192,216,240,..., dimensions={0} | all-to-all | bytes 196608 | tf_op jit(solution)/shard_map/all_to_all | solution.py:289
  116.3 0.7 broadcast_in_dim.32
  117.0 7.7 %all-to-all-start.3 = ((bf16[12,48,128]{2,1,0:T(8,128)(2,1)}), bf16[12,48,128]{2,1,0:T(8,128)(2,1)S(1)}, u32[]{:S(2)}, u32[]{:S(2)}) async-start(bf16[12,48,128]{2,1,0:T(8,128)(2,1)} %broadcast_in_dim.32), calls=%async_computation.3 | async-start | bytes 294912 | tf_op jit(solution)/shard_map/all_to_all | solution.py:289
  124.7 10.7 %all-to-all-done.3 = bf16[12,48,128]{2,1,0:T(8,128)(2,1)S(1)} async-done(((bf16[12,48,128]{2,1,0:T(8,128)(2,1)}), bf16[12,48,128]{2,1,0:T(8,128)(2,1)S(1)}, u32[]{:S(2)}, u32[]{:S(2)}) %all-to-all-start.3) | async-done | bytes 147488 | tf_op jit(solution)/shard_map/all_to_all | solution.py:289
  135.5 0.1 multiply_reduce_fusion
  135.6 0.8 add_sqrt_fusion
  136.4 0.1 divide_convert_fusion
  136.4 0.1 broadcast_in_dim.33
  136.5 14.8 %all_to_all.48 = bf16[32,48,128]{2,1,0:T(8,128)(2,1)S(1)} all-to-all(bf16[32,48,128]{2,1,0:T(8,128)(2,1)S(1)} %broadcast_in_dim.33), channel_id=1, replica_groups={{0,24,48,72,96,120,144,168,192,216,240,264,288,312,336,360,384,408,432,..., dimensions={0} | all-to-all | bytes 786432 | tf_op jit(solution)/shard_map/all_to_all | solution.py:289
  151.3 8.5 %collective-permute-start.4 = (bf16[1536,128]{1,0:T(8,128)(2,1)S(1)}, bf16[1536,128]{1,0:T(8,128)(2,1)S(1)}, u32[]{:S(2)}, u32[]{:S(2)}) collective-permute-start(bf16[1536,128]{1,0:T(8,128)(2,1)S(1)} %bitcast.16), channel_id=1, source_target_pairs={{0,12},{12,0},{24,36},{36,24},{48,60},{60,48},{72,84},{84,72},{96,... | collective-permute-start | bytes 1179656 | tf_op jit(solution)/shard_map/ppermute | solution.py:345
  159.8 0.1 copy.35.accum_ref
  160.0 0.6 reduce.2
  160.6 2.7 %shard_map.180 = f32[512,128]{1,0:T(8,128)} custom-call(s32[1,12]{1,0:T(1,128)S(1)} %copy-done.10, s32[12,256]{1,0:T(8,128)S(1)} %copy-done.8, bf16[3072,128]{1,0:T(8,128)(2,1)S(1)} %bitcast.14, bf16[512,128]{1,0:T(8,128)(2,1)S(1)} %copy-done.4, f32[512,1]{1,0:T(8,128)S(1)} %copy.35.accum_ref), custom_call_target="tpu_custom_call" | custom-call | flops 402653184 | bytes 2000000 | tf_op jit(solution)/shard_map/pallas_call | solution.py:283
  163.3 0.1 broadcast_select_fusion.1
  163.4 1.3 convert_subtract_fusion
  (36 shorter events, 0.1 us)
Async XLA Ops:
  0.6 20.6 %copy-start.1 = (s32[128,52]{0,1:T(8,128)S(1)}, s32[128,52]{0,1:T(8,128)}, u32[]{:S(2)}) copy-start(s32[128,52]{0,1:T(8,128)} %param.17) | copy-start | bytes 79876
  0.6 23.0 %copy-start = (bf16[3072,128]{1,0:T(8,128)(2,1)S(1)}, bf16[3072,128]{1,0:T(8,128)(2,1)}, u32[]{:S(2)}) copy-start(bf16[3072,128]{1,0:T(8,128)(2,1)} %table_ref.3) | copy-start | bytes 2359300
  0.7 23.0 %copy-start.2 = (bf16[512,256]{1,0:T(8,128)(2,1)S(1)}, bf16[512,256]{1,0:T(8,128)(2,1)}, u32[]{:S(2)}) copy-start(bf16[512,256]{1,0:T(8,128)(2,1)} %two_ref.1) | copy-start | bytes 786436
  0.7 1.0 copy-start.3
  1.7 0.7 copy-start.7
  2.4 0.7 copy-start.9
  3.0 18.4 %copy-start.18 = (bf16[128,13]{0,1:T(8,128)(2,1)S(1)}, bf16[128,13]{0,1:T(8,128)(2,1)}, u32[]{:S(2)}) copy-start(bf16[128,13]{0,1:T(8,128)(2,1)} %param.16) | copy-start | bytes 9988
  3.0 18.5 %copy-start.16 = (s32[12,256]{1,0:T(8,128)S(1)}, s32[12,256]{1,0:T(8,128)}, u32[]{:S(2)}) copy-start(s32[12,256]{1,0:T(8,128)} %bags_ref.1) | copy-start | bytes 36868
  3.0 19.3 %copy-start.20 = (f32[128]{0:T(128)S(1)}, f32[128]{0:T(128)}, u32[]{:S(2)}) copy-start(f32[128]{0:T(128)} %param.18) | copy-start | bytes 1540
  3.0 20.0 %copy-start.17 = (f32[3456]{0:T(1024)S(1)}, f32[3456]{0:T(1024)}, u32[]{:S(2)}) copy-start(f32[3456]{0:T(1024)} %param.31) | copy-start | bytes 41476
  3.0 20.6 %copy-start.5 = (bf16[256,128]{1,0:T(8,128)(2,1)S(1)}, bf16[256,128]{1,0:T(8,128)(2,1)}, u32[]{:S(2)}) copy-start(bf16[256,128]{1,0:T(8,128)(2,1)} %three_ref.1) | copy-start | bytes 196612
  3.1 20.6 %copy-start.6 = (bf16[13,512]{1,0:T(8,128)(2,1)S(1)}, bf16[13,512]{1,0:T(8,128)(2,1)}, u32[]{:S(2)}) copy-start(bf16[13,512]{1,0:T(8,128)(2,1)} %one_ref.1) | copy-start | bytes 39940
  5.6 43.9 %all-to-all-start = ((bf16[12,256,128]{2,1,0:T(8,128)(2,1)}), bf16[12,256,128]{2,1,0:T(8,128)(2,1)S(1)}, u32[]{:S(2)}, u32[]{:S(2)}) async-start(bf16[12,256,128]{2,1,0:T(8,128)(2,1)} %bitcast), calls=%async_computation | async-start | bytes 1572864 | tf_op jit(solution)/shard_map/all_to_all | solution.py:289
  38.9 1.2 copy-start.11
  40.2 0.6 copy-start.13
  49.4 0.9 copy-start.14
  66.6 35.5 %all-to-all-start.1 = ((bf16[12,256,128]{2,1,0:T(8,128)(2,1)}), bf16[12,256,128]{2,1,0:T(8,128)(2,1)S(1)}, u32[]{:S(2)}, u32[]{:S(2)}) async-start(bf16[12,256,128]{2,1,0:T(8,128)(2,1)} %bitcast.17), calls=%async_computation.1 | async-start | bytes 1572864 | tf_op jit(solution)/shard_map/all_to_all | solution.py:289
  74.2 1.2 copy-start.12
  81.1 4.3 %collective-permute-start = (bf16[1536,128]{1,0:T(8,128)(2,1)S(1)}, bf16[1536,128]{1,0:T(8,128)(2,1)S(1)}, u32[]{:S(2)}, u32[]{:S(2)}) collective-permute-start(bf16[1536,128]{1,0:T(8,128)(2,1)S(1)} %get-tuple-element.21), channel_id=1, source_target_pairs={{0,12},{12,0},{24,36},{36,24},{48,60},{60,48},{72,84},{84,72},{96,... | collective-permute-start | bytes 1179656 | tf_op jit(solution)/shard_map/ppermute | solution.py:329
  85.5 74.4 %copy-start.19 = (f32[512]{0:T(512)S(1)}, f32[512]{0:T(512)}, u32[]{:S(2)}) copy-start(f32[512]{0:T(512)} %param.22) | copy-start | bytes 6148
  85.5 74.5 %copy-start.15 = (f32[128,1]{1,0:T(8,128)S(1)}, f32[128,1]{1,0:T(8,128)}, u32[]{:S(2)}) copy-start(f32[128,1]{1,0:T(8,128)} %get-tuple-element.18) | copy-start | bytes 1540
  85.5 75.1 %copy-start.4 = (bf16[512,128]{1,0:T(8,128)(2,1)S(1)}, bf16[512,128]{1,0:T(8,128)(2,1)}, u32[]{:S(2)}) copy-start(bf16[512,128]{1,0:T(8,128)(2,1)} %table_ref.5) | copy-start | bytes 393220
  85.5 75.1 %copy-start.8 = (s32[12,256]{1,0:T(8,128)S(1)}, s32[12,256]{1,0:T(8,128)}, u32[]{:S(2)}) copy-start(s32[12,256]{1,0:T(8,128)} %rows_ref.3) | copy-start | bytes 36868
  85.5 75.1 %copy-start.10 = (s32[1,12]{1,0:T(1,128)S(1)}, s32[1,12]{1,0:T(1,128)}, u32[]{:S(2)}) copy-start(s32[1,12]{1,0:T(1,128)} %count_ref.3) | copy-start | bytes 148
  85.5 9.5 %collective-permute-start.3 = (bf16[384,128]{1,0:T(8,128)(2,1)S(1)}, bf16[384,128]{1,0:T(8,128)(2,1)S(1)}, u32[]{:S(2)}, u32[]{:S(2)}) collective-permute-start(bf16[384,128]{1,0:T(8,128)(2,1)S(1)} %get-tuple-element.25), channel_id=1, source_target_pairs={{0,576},{12,588},{24,600},{36,612},{48,624},{60,636},{72,648},{84,... | collective-permute-start | bytes 294920 | tf_op jit(solution)/shard_map/ppermute | solution.py:333
  90.1 6.9 %collective-permute-start.2 = (bf16[384,128]{1,0:T(8,128)(2,1)S(1)}, bf16[384,128]{1,0:T(8,128)(2,1)S(1)}, u32[]{:S(2)}, u32[]{:S(2)}) collective-permute-start(bf16[384,128]{1,0:T(8,128)(2,1)S(1)} %get-tuple-element.24), channel_id=1, source_target_pairs={{0,384},{12,396},{24,408},{36,420},{48,432},{60,444},{72,456},{84,... | collective-permute-start | bytes 294920 | tf_op jit(solution)/shard_map/ppermute | solution.py:333
  92.5 6.7 %collective-permute-start.1 = (bf16[384,128]{1,0:T(8,128)(2,1)S(1)}, bf16[384,128]{1,0:T(8,128)(2,1)S(1)}, u32[]{:S(2)}, u32[]{:S(2)}) collective-permute-start(bf16[384,128]{1,0:T(8,128)(2,1)S(1)} %get-tuple-element.23), channel_id=1, source_target_pairs={{0,192},{12,204},{24,216},{36,228},{48,240},{60,252},{72,264},{84,... | collective-permute-start | bytes 294920 | tf_op jit(solution)/shard_map/ppermute | solution.py:333
  117.0 18.4 %all-to-all-start.3 = ((bf16[12,48,128]{2,1,0:T(8,128)(2,1)}), bf16[12,48,128]{2,1,0:T(8,128)(2,1)S(1)}, u32[]{:S(2)}, u32[]{:S(2)}) async-start(bf16[12,48,128]{2,1,0:T(8,128)(2,1)} %broadcast_in_dim.32), calls=%async_computation.3 | async-start | bytes 294912 | tf_op jit(solution)/shard_map/all_to_all | solution.py:289
  151.3 11.9 %collective-permute-start.4 = (bf16[1536,128]{1,0:T(8,128)(2,1)S(1)}, bf16[1536,128]{1,0:T(8,128)(2,1)S(1)}, u32[]{:S(2)}, u32[]{:S(2)}) collective-permute-start(bf16[1536,128]{1,0:T(8,128)(2,1)S(1)} %bitcast.16), channel_id=1, source_target_pairs={{0,12},{12,0},{24,36},{36,24},{48,60},{60,48},{72,84},{84,72},{96,... | collective-permute-start | bytes 1179656 | tf_op jit(solution)/shard_map/ppermute | solution.py:345

commit v3 on v2

--- a/solution.py
+++ b/solution.py
@@ -226,7 +226,7 @@
 
 
 def pick(count, rows_t, table):
-    return call(pick_kernel, sds((SLOTS, E), bf), [SM, VM, VM], [pltpu.VMEM((ROWS // 2, 2 * E), bf)], 2 * SLOTS * ROWS * E, 2000000)(
+    return call(pick_kernel, sds((SLOTS, E), bf), [SM, VM, VM], [pltpu.VMEM((ROWS // 2, 2 * E), bf)], 2 * SLOTS * ROWS * E, 2000000, 62)(
         count, rows_t, table
     )
 
@@ -310,8 +310,8 @@
     n_dp = lax.axis_size("dp")
     n_xy = n_dp // 2
     n_y = n_xy // 4
-    xy_groups = [[2 * k + c for k in range(n_xy)] for c in range(2)]
-    y_groups = [[2 * n_y * x + 2 * y + c for y in range(n_y)] for x in range(4) for c in range(2)]
+    whole = [[(2 * k + c) * NT + z for k in range(n_xy) for z in range(NT)] for c in range(2)]
+    slab = [g[n_y * NT * x : n_y * NT * (x + 1)] for g in whole for x in range(4)]
     twin = [(i, i ^ 1) for i in range(n_dp)]
     outgoing = pick(send_count, send_rows, cold_table)
     arrived = a2a(outgoing, "table")
@@ -332,21 +332,21 @@
         ahead = [(i, (i + 2 * n_y * k) % n_dp) for i in range(n_dp)]
         total = total + lax.ppermute(parts[k - 1], "dp", ahead).astype(f32)
     total, returned = lax.optimization_barrier((total.astype(bf), returned))
-    share = half // n_xy
-    line = a2a(total, "dp", y_groups)
-    plane = jnp.sum(line.reshape(n_y, share, E).astype(f32), axis=0).astype(bf)
-    column = a2a(jnp.broadcast_to(plane[None], (NT, share, E)).reshape(NT * share, E), "table")
-    grad = jnp.sum(column.reshape(NT, share, E).astype(f32), axis=0)
-    first = core * half + lax.div(lax.axis_index("dp"), 2) * share
+    share = half // (n_xy * NT)
+    both = ("dp", "table")
+    column = a2a(total, both, slab)
+    new_cold = cold_update(send_count, send_rows, returned, cold_table, cold_accum[:, None])
+    column, new_cold = lax.optimization_barrier((column, new_cold))
+    grad = jnp.sum(column.reshape(n_y * NT, share, E).astype(f32), axis=0)
+    first = core * half + (lax.div(lax.axis_index("dp"), 2) * NT + lax.axis_index("table")) * share
     accum = lax.dynamic_slice_in_dim(hot_accum, first, share, 0)
     step = grad / jnp.sqrt(accum + jnp.mean(grad * grad, axis=1))[:, None]
     step = step.astype(bf)
-    steps = a2a(jnp.broadcast_to(step[None], (n_xy, share, E)).reshape(half, E), "dp", xy_groups)
+    steps = a2a(jnp.broadcast_to(step[None], (n_xy * NT, share, E)).reshape(half, E), both, whole)
     others = lax.ppermute(steps, "dp", twin)
     low = jnp.where(core == 0, steps, others)
     high = jnp.where(core == 0, others, steps)
     new_hot = hot_table.astype(f32) - jnp.concatenate([low, high], axis=0).astype(f32)
-    new_cold = cold_update(send_count, send_rows, returned, cold_table, cold_accum[:, None])
     return (logits[:, 0], new_hot, new_cold)
 
 

time: 165 us -> 174 us (1.055)
  starting transfers between devices: 51.9 us -> 58 us
  blocking collectives: 29 us -> 33.1 us
  local copies, waits for them, and re-layouts: 9.51 us -> 6.53 us
    all_to_all x3, starting transfers between devices: 31 us -> 37.9 us  [a2a(): lax.all_to_all(v, axis, split_axis=0, concat_axis=0, tiled=True, axis_ind...]
    all_to_all x2 -> x1, blocking collectives: 29 us -> 33.1 us  [a2a(): lax.all_to_all(v, axis, split_axis=0, concat_axis=0, tiled=True, axis_ind...]
    unnamed x45 -> x39, local copies, waits for them, and re-layouts: 7.29 us -> 4.94 us
  transfers between devices with their start and end apart: 8 -> 8, of which waited for: 6 -> 7; matrix products, arithmetic and copies ran while one was open for 2% -> 2% of each run, Pallas kernels for 14% -> 14%
where the time goes in v3:
time: 174 us; the launch traced here: 173 us
  starting transfers between devices  58 us (33%)
  Pallas kernels  43 us (25%)
  blocking collectives  33.1 us (19%)
  waiting for transfers between devices  27.5 us (16%)
  local copies, waits for them, and re-layouts  6.53 us (4%)
  other arithmetic  3.74 us (2%)
    all_to_all x3, starting transfers between devices, a2a(): lax.all_to_all(v, axis, split_axis=0, concat_axis=0, tiled=True, axis_ind...  37.9 us
    all_to_all x1, blocking collectives, a2a(): lax.all_to_all(v, axis, split_axis=0, concat_axis=0, tiled=True, axis_ind...  33.1 us
    all_to_all x3, waiting for transfers between devices, a2a(): lax.all_to_all(v, axis, split_axis=0, concat_axis=0, tiled=True, axis_ind...  21.3 us
    pallas_call x1, Pallas kernels, cross(): call(cross_kernel, (sds((B, 1), f32), sds((HB, 2 * E), bf), sds((SLOTS, E...  16.3 us
    pallas_call x1, Pallas kernels, hot_pool(): call(hot_kernel, (sds((BAGS, E), f32), sds((B, E), bf)), [VM] * 6, (), 2...  15.2 us
    ppermute x3, starting transfers between devices, body(): total = total + lax.ppermute(parts[k - 1], 'dp', ahead).astype(f32)  9.33 us
    ppermute x1, starting transfers between devices, body(): others = lax.ppermute(steps, 'dp', twin)  7.69 us
    pallas_call x1, Pallas kernels, hot_sum(): call(hot_grad_kernel, (sds((HOT // 2, E), f32), sds((HOT // 2, E), bf)),...  5.72 us
  transfers between devices with their start and end apart: 8, of which 7 were waited for; matrix products, arithmetic and copies ran while one was open for 2% of the time, Pallas kernels for 14%

profile of v3, /device:TPU:1, one launch (start us, length us, event | category | flops | bytes accessed | tf_op | source)
XLA Modules:
  0.0 172.9 jit_solution(746361397975328014)
XLA Ops:
  0.7 0.0 copy-start.13
  0.7 3.0 %shard_map.176 = bf16[3072,128]{1,0:T(8,128)(2,1)} custom-call(s32[1,12]{1,0:T(1,128)} %count_ref.3, s32[12,256]{1,0:T(8,128)} %rows_ref.3, bf16[512,128]{1,0:T(8,128)(2,1)} %table_ref.5), custom_call_target="tpu_custom_call" | custom-call | flops 402653184 | bytes 2000000 | tf_op jit(solution)/shard_map/pallas_call | solution.py:229
  3.7 15.7 %all-to-all-start = ((bf16[12,256,128]{2,1,0:T(8,128)(2,1)}), bf16[12,256,128]{2,1,0:T(8,128)(2,1)S(1)}, u32[]{:S(2)}, u32[]{:S(2)}) async-start(bf16[12,256,128]{2,1,0:T(8,128)(2,1)} %bitcast.21), calls=%async_computation | async-start | bytes 1572864 | tf_op jit(solution)/shard_map/all_to_all | solution.py:289
  19.4 0.1 copy.24.ids_ref
  19.5 0.1 copy.25.dense_ref
  19.7 0.8 copy.26
  20.4 0.7 copy.27.grad_ref
  21.2 0.6 broadcast_in_dim.23.head_ref
  21.8 15.2 %shard_map.175 = (f32[3328,128]{1,0:T(8,128)S(1)}, bf16[128,128]{1,0:T(8,128)(2,1)S(1)}) custom-call(s32[128,128]{1,0:T(8,128)S(1)} %pad.4.ids_ref, bf16[3072,128]{1,0:T(8,128)(2,1)S(1)} %copy-done, bf16[128,13]{1,0:T(8,128)(2,1)S(1)} %copy.25.dense_ref, bf16[13,512]{1,0:T(8,128)(2,1)S(1)} %copy-done.5, bf16[512,256]{1,0:T(8,128)(2,1)S(1)} %copy-done.2, ...), custom_call_target="tpu_custom_call" | custom-call | flops 2617245696 | bytes 4000000 | tf_op jit(solution)/shard_map/pallas_call | solution.py:235
  37.1 1.2 copy-done.8
  38.3 0.6 copy-done.10
  38.9 8.6 %all-to-all-done = bf16[12,256,128]{2,1,0:T(8,128)(2,1)S(1)} async-done(((bf16[12,256,128]{2,1,0:T(8,128)(2,1)}), bf16[12,256,128]{2,1,0:T(8,128)(2,1)S(1)}, u32[]{:S(2)}, u32[]{:S(2)}) %all-to-all-start) | async-done | bytes 786464 | tf_op jit(solution)/shard_map/all_to_all | solution.py:289
  47.6 0.9 copy-done.11
  48.4 16.3 %shard_map.177 = (f32[128,1]{1,0:T(8,128)}, bf16[1664,256]{1,0:T(8,128)(2,1)}, bf16[3072,128]{1,0:T(8,128)(2,1)}) custom-call(f32[3328,128]{1,0:T(8,128)} %copy-done.8, bf16[128,128]{1,0:T(8,128)(2,1)} %copy-done.10, bf16[3072,128]{1,0:T(8,128)(2,1)} %bitcast.20, s32[12,256]{1,0:T(8,128)} %bags_ref.1, s32[256,12]{1,0:T(8,128)} %bitcast.22, ...), custom_call_target="tpu_custom_call" | custom-call | flops 7046430720 | bytes 14000000 | tf_op jit(solution)/shard_map/pallas_call | solution.py:241
  64.8 7.6 %all-to-all-start.1 = ((bf16[12,256,128]{2,1,0:T(8,128)(2,1)}), bf16[12,256,128]{2,1,0:T(8,128)(2,1)S(1)}, u32[]{:S(2)}, u32[]{:S(2)}) async-start(bf16[12,256,128]{2,1,0:T(8,128)(2,1)} %bitcast.19), calls=%async_computation.1 | async-start | bytes 1572864 | tf_op jit(solution)/shard_map/all_to_all | solution.py:289
  72.4 0.0 copy-start.9
  72.4 1.1 copy-done.9
  73.5 5.7 %shard_map.178 = (f32[1536,128]{1,0:T(8,128)S(1)}, bf16[1536,128]{1,0:T(8,128)(2,1)S(1)}) custom-call(s32[1]{0:T(128)} %bitcast.5.core_ref, bf16[1664,256]{1,0:T(8,128)(2,1)S(1)} %copy-done.9, s32[128,52]{1,0:T(8,128)S(1)} %copy.24.ids_ref, s32[52,128]{1,0:T(8,128)S(1)} %bitcast.16), custom_call_target="tpu_custom_call" | custom-call | flops 2617245696 | bytes 3000000 | tf_op jit(solution)/shard_map/pallas_call | solution.py:259
  79.2 0.0 copy-start.16
  79.3 0.0 copy-start.3
  79.3 0.0 copy-start.6
  79.3 0.0 copy-start.7
  79.3 3.1 %collective-permute-start = (bf16[1536,128]{1,0:T(8,128)(2,1)S(1)}, bf16[1536,128]{1,0:T(8,128)(2,1)S(1)}, u32[]{:S(2)}, u32[]{:S(2)}) collective-permute-start(bf16[1536,128]{1,0:T(8,128)(2,1)S(1)} %get-tuple-element.23), channel_id=1, source_target_pairs={{0,12},{12,0},{24,36},{36,24},{48,60},{60,48},{72,84},{84,72},{96,... | collective-permute-start | bytes 1179656 | tf_op jit(solution)/shard_map/ppermute | solution.py:329
  82.4 1.3 collective-permute-done.met_ref
  83.7 0.1 shard_map.179
  83.8 4.4 %collective-permute-start.3 = (bf16[384,128]{1,0:T(8,128)(2,1)S(1)}, bf16[384,128]{1,0:T(8,128)(2,1)S(1)}, u32[]{:S(2)}, u32[]{:S(2)}) collective-permute-start(bf16[384,128]{1,0:T(8,128)(2,1)S(1)} %get-tuple-element.27), channel_id=1, source_target_pairs={{0,576},{12,588},{24,600},{36,612},{48,624},{60,636},{72,648},{84,... | collective-permute-start | bytes 294920 | tf_op jit(solution)/shard_map/ppermute | solution.py:333
  88.2 2.4 %collective-permute-start.2 = (bf16[384,128]{1,0:T(8,128)(2,1)S(1)}, bf16[384,128]{1,0:T(8,128)(2,1)S(1)}, u32[]{:S(2)}, u32[]{:S(2)}) collective-permute-start(bf16[384,128]{1,0:T(8,128)(2,1)S(1)} %get-tuple-element.26), channel_id=1, source_target_pairs={{0,384},{12,396},{24,408},{36,420},{48,432},{60,444},{72,456},{84,... | collective-permute-start | bytes 294920 | tf_op jit(solution)/shard_map/ppermute | solution.py:333
  90.6 2.5 %collective-permute-start.1 = (bf16[384,128]{1,0:T(8,128)(2,1)S(1)}, bf16[384,128]{1,0:T(8,128)(2,1)S(1)}, u32[]{:S(2)}, u32[]{:S(2)}) collective-permute-start(bf16[384,128]{1,0:T(8,128)(2,1)S(1)} %get-tuple-element.25), channel_id=1, source_target_pairs={{0,192},{12,204},{24,216},{36,228},{48,240},{60,252},{72,264},{84,... | collective-permute-start | bytes 294920 | tf_op jit(solution)/shard_map/ppermute | solution.py:333
  93.2 0.0 collective-permute-done.3
  93.2 1.9 %collective-permute-done.2 = bf16[384,128]{1,0:T(8,128)(2,1)S(1)} collective-permute-done((bf16[384,128]{1,0:T(8,128)(2,1)S(1)}, bf16[384,128]{1,0:T(8,128)(2,1)S(1)}, u32[]{:S(2)}, u32[]{:S(2)}) %collective-permute-start.2) | collective-permute-done | bytes 98336 | tf_op jit(solution)/shard_map/ppermute | solution.py:333
  95.1 2.3 %collective-permute-done.1 = bf16[384,128]{1,0:T(8,128)(2,1)S(1)} collective-permute-done((bf16[384,128]{1,0:T(8,128)(2,1)S(1)}, bf16[384,128]{1,0:T(8,128)(2,1)S(1)}, u32[]{:S(2)}, u32[]{:S(2)}) %collective-permute-start.1) | collective-permute-done | bytes 98336 | tf_op jit(solution)/shard_map/ppermute | solution.py:333
  97.4 0.7 add_convert_fusion
  98.1 2.2 %all-to-all-done.1 = bf16[12,256,128]{2,1,0:T(8,128)(2,1)S(1)} async-done(((bf16[12,256,128]{2,1,0:T(8,128)(2,1)}), bf16[12,256,128]{2,1,0:T(8,128)(2,1)S(1)}, u32[]{:S(2)}, u32[]{:S(2)}) %all-to-all-start.1) | async-done | bytes 786464 | tf_op jit(solution)/shard_map/all_to_all | solution.py:289
  100.2 14.6 %all-to-all-start.2 = ((bf16[96,4,128]{2,1,0:T(4,128)(2,1)}), bf16[96,4,128]{2,1,0:T(4,128)(2,1)S(1)}, u32[]{:S(2)}, u32[]{:S(2)}) async-start(bf16[96,4,128]{2,1,0:T(4,128)(2,1)} %bitcast.9), calls=%async_computation.2 | async-start | bytes 196608 | tf_op jit(solution)/shard_map/all_to_all | solution.py:289
  114.9 0.1 copy.29.accum_ref
  115.1 2.7 %shard_map.180 = f32[512,128]{1,0:T(8,128)} custom-call(s32[1,12]{1,0:T(1,128)S(1)} %copy-done.7, s32[12,256]{1,0:T(8,128)S(1)} %copy-done.6, bf16[3072,128]{1,0:T(8,128)(2,1)S(1)} %bitcast.15, bf16[512,128]{1,0:T(8,128)(2,1)S(1)} %copy-done.3, f32[512,1]{1,0:T(8,128)S(1)} %copy.29.accum_ref), custom_call_target="tpu_custom_call" | custom-call | flops 402653184 | bytes 2000000 | tf_op jit(solution)/shard_map/pallas_call | solution.py:283
  117.8 10.5 %all-to-all-done.2 = bf16[96,4,128]{2,1,0:T(4,128)(2,1)S(1)} async-done(((bf16[96,4,128]{2,1,0:T(4,128)(2,1)}), bf16[96,4,128]{2,1,0:T(4,128)(2,1)S(1)}, u32[]{:S(2)}, u32[]{:S(2)}) %all-to-all-start.2) | async-done | bytes 98336 | tf_op jit(solution)/shard_map/all_to_all | solution.py:289
  128.3 0.1 convert_reduce_fusion
  128.4 0.1 multiply_reduce_fusion
  128.5 0.8 add_sqrt_fusion
  129.2 0.1 divide_convert_fusion
  129.3 0.1 broadcast_in_dim.27
  129.4 33.1 %all_to_all.44 = bf16[384,4,128]{2,1,0:T(4,128)(2,1)S(1)} all-to-all(bf16[384,4,128]{2,1,0:T(4,128)(2,1)S(1)} %broadcast_in_dim.27), channel_id=1, replica_groups={{0,1,2,3,4,5,6,7,8,9,10,11,24,25,26,27,28,29,30,31,32,33,34,35,48,49,50..., dimensions={0} | all-to-all | bytes 786432 | tf_op jit(solution)/shard_map/all_to_all | solution.py:289
  162.5 7.7 %collective-permute-start.4 = (bf16[1536,128]{1,0:T(8,128)(2,1)S(1)}, bf16[1536,128]{1,0:T(8,128)(2,1)S(1)}, u32[]{:S(2)}, u32[]{:S(2)}) collective-permute-start(bf16[1536,128]{1,0:T(8,128)(2,1)S(1)} %bitcast.17), channel_id=1, source_target_pairs={{0,12},{12,0},{24,36},{36,24},{48,60},{60,48},{72,84},{84,72},{96,... | collective-permute-start | bytes 1179656 | tf_op jit(solution)/shard_map/ppermute | solution.py:346
  170.2 0.6 reduce
  170.9 0.7 collective-permute-done.4
  171.5 0.1 broadcast_select_fusion.1
  171.6 1.3 convert_subtract_fusion
  (27 shorter events, 0.1 us)
Async XLA Ops:
  0.6 18.8 %copy-start.1 = (s32[128,52]{0,1:T(8,128)S(1)}, s32[128,52]{0,1:T(8,128)}, u32[]{:S(2)}) copy-start(s32[128,52]{0,1:T(8,128)} %param.17) | copy-start | bytes 79876
  0.6 18.9 %copy-start.15 = (bf16[128,13]{0,1:T(8,128)(2,1)S(1)}, bf16[128,13]{0,1:T(8,128)(2,1)}, u32[]{:S(2)}) copy-start(bf16[128,13]{0,1:T(8,128)(2,1)} %param.16) | copy-start | bytes 9988
  0.7 19.0 %copy-start.13 = (s32[12,256]{1,0:T(8,128)S(1)}, s32[12,256]{1,0:T(8,128)}, u32[]{:S(2)}) copy-start(s32[12,256]{1,0:T(8,128)} %bags_ref.1) | copy-start | bytes 36868
  0.7 19.8 %copy-start.17 = (f32[128]{0:T(128)S(1)}, f32[128]{0:T(128)}, u32[]{:S(2)}) copy-start(f32[128]{0:T(128)} %param.18) | copy-start | bytes 1540
  0.7 20.5 %copy-start.14 = (f32[3456]{0:T(1024)S(1)}, f32[3456]{0:T(1024)}, u32[]{:S(2)}) copy-start(f32[3456]{0:T(1024)} %param.31) | copy-start | bytes 41476
  0.7 21.1 %copy-start = (bf16[3072,128]{1,0:T(8,128)(2,1)S(1)}, bf16[3072,128]{1,0:T(8,128)(2,1)}, u32[]{:S(2)}) copy-start(bf16[3072,128]{1,0:T(8,128)(2,1)} %table_ref.3) | copy-start | bytes 2359300
  0.7 21.1 %copy-start.5 = (bf16[13,512]{1,0:T(8,128)(2,1)S(1)}, bf16[13,512]{1,0:T(8,128)(2,1)}, u32[]{:S(2)}) copy-start(bf16[13,512]{1,0:T(8,128)(2,1)} %one_ref.1) | copy-start | bytes 39940
  0.7 21.1 %copy-start.2 = (bf16[512,256]{1,0:T(8,128)(2,1)S(1)}, bf16[512,256]{1,0:T(8,128)(2,1)}, u32[]{:S(2)}) copy-start(bf16[512,256]{1,0:T(8,128)(2,1)} %two_ref.1) | copy-start | bytes 786436
  0.7 21.1 %copy-start.4 = (bf16[256,128]{1,0:T(8,128)(2,1)S(1)}, bf16[256,128]{1,0:T(8,128)(2,1)}, u32[]{:S(2)}) copy-start(bf16[256,128]{1,0:T(8,128)(2,1)} %three_ref.1) | copy-start | bytes 196612
  3.7 43.9 %all-to-all-start = ((bf16[12,256,128]{2,1,0:T(8,128)(2,1)}), bf16[12,256,128]{2,1,0:T(8,128)(2,1)S(1)}, u32[]{:S(2)}, u32[]{:S(2)}) async-start(bf16[12,256,128]{2,1,0:T(8,128)(2,1)} %bitcast.21), calls=%async_computation | async-start | bytes 1572864 | tf_op jit(solution)/shard_map/all_to_all | solution.py:289
  37.1 1.2 copy-start.8
  38.3 0.6 copy-start.10
  47.6 0.9 copy-start.11
  64.8 35.5 %all-to-all-start.1 = ((bf16[12,256,128]{2,1,0:T(8,128)(2,1)}), bf16[12,256,128]{2,1,0:T(8,128)(2,1)S(1)}, u32[]{:S(2)}, u32[]{:S(2)}) async-start(bf16[12,256,128]{2,1,0:T(8,128)(2,1)} %bitcast.19), calls=%async_computation.1 | async-start | bytes 1572864 | tf_op jit(solution)/shard_map/all_to_all | solution.py:289
  72.4 1.2 copy-start.9
  79.2 35.7 %copy-start.16 = (f32[512]{0:T(512)S(1)}, f32[512]{0:T(512)}, u32[]{:S(2)}) copy-start(f32[512]{0:T(512)} %param.22) | copy-start | bytes 6148
  79.3 35.8 %copy-start.3 = (bf16[512,128]{1,0:T(8,128)(2,1)S(1)}, bf16[512,128]{1,0:T(8,128)(2,1)}, u32[]{:S(2)}) copy-start(bf16[512,128]{1,0:T(8,128)(2,1)} %table_ref.5) | copy-start | bytes 393220
  79.3 35.8 %copy-start.6 = (s32[12,256]{1,0:T(8,128)S(1)}, s32[12,256]{1,0:T(8,128)}, u32[]{:S(2)}) copy-start(s32[12,256]{1,0:T(8,128)} %rows_ref.3) | copy-start | bytes 36868
  79.3 35.8 %copy-start.7 = (s32[1,12]{1,0:T(1,128)S(1)}, s32[1,12]{1,0:T(1,128)}, u32[]{:S(2)}) copy-start(s32[1,12]{1,0:T(1,128)} %count_ref.3) | copy-start | bytes 148
  79.3 4.4 %collective-permute-start = (bf16[1536,128]{1,0:T(8,128)(2,1)S(1)}, bf16[1536,128]{1,0:T(8,128)(2,1)S(1)}, u32[]{:S(2)}, u32[]{:S(2)}) collective-permute-start(bf16[1536,128]{1,0:T(8,128)(2,1)S(1)} %get-tuple-element.23), channel_id=1, source_target_pairs={{0,12},{12,0},{24,36},{36,24},{48,60},{60,48},{72,84},{84,72},{96,... | collective-permute-start | bytes 1179656 | tf_op jit(solution)/shard_map/ppermute | solution.py:329
  83.8 9.4 %collective-permute-start.3 = (bf16[384,128]{1,0:T(8,128)(2,1)S(1)}, bf16[384,128]{1,0:T(8,128)(2,1)S(1)}, u32[]{:S(2)}, u32[]{:S(2)}) collective-permute-start(bf16[384,128]{1,0:T(8,128)(2,1)S(1)} %get-tuple-element.27), channel_id=1, source_target_pairs={{0,576},{12,588},{24,600},{36,612},{48,624},{60,636},{72,648},{84,... | collective-permute-start | bytes 294920 | tf_op jit(solution)/shard_map/ppermute | solution.py:333
  88.2 6.9 %collective-permute-start.2 = (bf16[384,128]{1,0:T(8,128)(2,1)S(1)}, bf16[384,128]{1,0:T(8,128)(2,1)S(1)}, u32[]{:S(2)}, u32[]{:S(2)}) collective-permute-start(bf16[384,128]{1,0:T(8,128)(2,1)S(1)} %get-tuple-element.26), channel_id=1, source_target_pairs={{0,384},{12,396},{24,408},{36,420},{48,432},{60,444},{72,456},{84,... | collective-permute-start | bytes 294920 | tf_op jit(solution)/shard_map/ppermute | solution.py:333
  90.6 6.7 %collective-permute-start.1 = (bf16[384,128]{1,0:T(8,128)(2,1)S(1)}, bf16[384,128]{1,0:T(8,128)(2,1)S(1)}, u32[]{:S(2)}, u32[]{:S(2)}) collective-permute-start(bf16[384,128]{1,0:T(8,128)(2,1)S(1)} %get-tuple-element.25), channel_id=1, source_target_pairs={{0,192},{12,204},{24,216},{36,228},{48,240},{60,252},{72,264},{84,... | collective-permute-start | bytes 294920 | tf_op jit(solution)/shard_map/ppermute | solution.py:333
  100.2 28.0 %all-to-all-start.2 = ((bf16[96,4,128]{2,1,0:T(4,128)(2,1)}), bf16[96,4,128]{2,1,0:T(4,128)(2,1)S(1)}, u32[]{:S(2)}, u32[]{:S(2)}) async-start(bf16[96,4,128]{2,1,0:T(4,128)(2,1)} %bitcast.9), calls=%async_computation.2 | async-start | bytes 196608 | tf_op jit(solution)/shard_map/all_to_all | solution.py:289
  114.9 55.4 %copy-start.12 = (f32[128,1]{1,0:T(8,128)S(1)}, f32[128,1]{1,0:T(8,128)}, u32[]{:S(2)}) copy-start(f32[128,1]{1,0:T(8,128)} %get-tuple-element.20) | copy-start | bytes 1540
  162.5 9.0 %collective-permute-start.4 = (bf16[1536,128]{1,0:T(8,128)(2,1)S(1)}, bf16[1536,128]{1,0:T(8,128)(2,1)S(1)}, u32[]{:S(2)}, u32[]{:S(2)}) collective-permute-start(bf16[1536,128]{1,0:T(8,128)(2,1)S(1)} %bitcast.17), channel_id=1, source_target_pairs={{0,12},{12,0},{24,36},{36,24},{48,60},{60,48},{72,84},{84,72},{96,... | collective-permute-start | bytes 1179656 | tf_op jit(solution)/shard_map/ppermute | solution.py:346

commit v4 on v2

--- a/solution.py
+++ b/solution.py
@@ -226,7 +226,7 @@
 
 
 def pick(count, rows_t, table):
-    return call(pick_kernel, sds((SLOTS, E), bf), [SM, VM, VM], [pltpu.VMEM((ROWS // 2, 2 * E), bf)], 2 * SLOTS * ROWS * E, 2000000)(
+    return call(pick_kernel, sds((SLOTS, E), bf), [SM, VM, VM], [pltpu.VMEM((ROWS // 2, 2 * E), bf)], 2 * SLOTS * ROWS * E, 2000000, 62)(
         count, rows_t, table
     )
 
@@ -336,6 +336,8 @@
     line = a2a(total, "dp", y_groups)
     plane = jnp.sum(line.reshape(n_y, share, E).astype(f32), axis=0).astype(bf)
     column = a2a(jnp.broadcast_to(plane[None], (NT, share, E)).reshape(NT * share, E), "table")
+    new_cold = cold_update(send_count, send_rows, returned, cold_table, cold_accum[:, None])
+    column, new_cold = lax.optimization_barrier((column, new_cold))
     grad = jnp.sum(column.reshape(NT, share, E).astype(f32), axis=0)
     first = core * half + lax.div(lax.axis_index("dp"), 2) * share
     accum = lax.dynamic_slice_in_dim(hot_accum, first, share, 0)
@@ -346,7 +348,6 @@
     low = jnp.where(core == 0, steps, others)
     high = jnp.where(core == 0, others, steps)
     new_hot = hot_table.astype(f32) - jnp.concatenate([low, high], axis=0).astype(f32)
-    new_cold = cold_update(send_count, send_rows, returned, cold_table, cold_accum[:, None])
     return (logits[:, 0], new_hot, new_cold)
 
 

time: 165 us -> 161 us (0.976)
  local copies, waits for them, and re-layouts: 9.51 us -> 7.18 us
  waiting for transfers between devices: 27.7 us -> 25.5 us
    all_to_all x3, waiting for transfers between devices: 22.2 us -> 19.3 us  [a2a(): lax.all_to_all(v, axis, split_axis=0, concat_axis=0, tiled=True, axis_ind...]
    unnamed x45 -> x39, local copies, waits for them, and re-layouts: 7.29 us -> 4.95 us
  transfers between devices with their start and end apart: 8 -> 8, of which waited for: 6 -> 7; matrix products, arithmetic and copies ran while one was open for 2% -> 2% of each run, Pallas kernels for 14% -> 15%
where the time goes in v4:
time: 161 us
  starting transfers between devices  51.9 us (32%)
  Pallas kernels  43 us (27%)
  blocking collectives  29 us (18%)
  waiting for transfers between devices  25.5 us (16%)
  local copies, waits for them, and re-layouts  7.18 us (4%)
  other arithmetic  3.08 us (2%)
    all_to_all x3, starting transfers between devices, a2a(): lax.all_to_all(v, axis, split_axis=0, concat_axis=0, tiled=True, axis_ind...  31 us
    all_to_all x2, blocking collectives, a2a(): lax.all_to_all(v, axis, split_axis=0, concat_axis=0, tiled=True, axis_ind...  29 us
    all_to_all x3, waiting for transfers between devices, a2a(): lax.all_to_all(v, axis, split_axis=0, concat_axis=0, tiled=True, axis_ind...  19.3 us
    pallas_call x1, Pallas kernels, cross(): call(cross_kernel, (sds((B, 1), f32), sds((HB, 2 * E), bf), sds((SLOTS, E...  16.3 us
    pallas_call x1, Pallas kernels, hot_pool(): call(hot_kernel, (sds((BAGS, E), f32), sds((B, E), bf)), [VM] * 6, (), 2...  15.2 us
    ppermute x3, starting transfers between devices, body(): total = total + lax.ppermute(parts[k - 1], 'dp', ahead).astype(f32)  9.33 us
    ppermute x1, starting transfers between devices, body(): others = lax.ppermute(steps, 'dp', twin)  8.47 us
    pallas_call x1, Pallas kernels, hot_sum(): call(hot_grad_kernel, (sds((HOT // 2, E), f32), sds((HOT // 2, E), bf)),...  5.72 us
  transfers between devices with their start and end apart: 8, of which 7 were waited for; matrix products, arithmetic and copies ran while one was open for 2% of the time, Pallas kernels for 15%

profile of v4, /device:TPU:1, one launch (start us, length us, event | category | flops | bytes accessed | tf_op | source)
XLA Modules:
  0.0 160.7 jit_solution(16472134848676612122)
XLA Ops:
  0.7 0.0 copy-start.13
  0.7 3.0 %shard_map.176 = bf16[3072,128]{1,0:T(8,128)(2,1)} custom-call(s32[1,12]{1,0:T(1,128)} %count_ref.3, s32[12,256]{1,0:T(8,128)} %rows_ref.3, bf16[512,128]{1,0:T(8,128)(2,1)} %table_ref.5), custom_call_target="tpu_custom_call" | custom-call | flops 402653184 | bytes 2000000 | tf_op jit(solution)/shard_map/pallas_call | solution.py:229
  3.7 15.7 %all-to-all-start = ((bf16[12,256,128]{2,1,0:T(8,128)(2,1)}), bf16[12,256,128]{2,1,0:T(8,128)(2,1)S(1)}, u32[]{:S(2)}, u32[]{:S(2)}) async-start(bf16[12,256,128]{2,1,0:T(8,128)(2,1)} %bitcast.22), calls=%async_computation | async-start | bytes 1572864 | tf_op jit(solution)/shard_map/all_to_all | solution.py:289
  19.4 0.1 copy.30.ids_ref
  19.5 0.1 copy.31.dense_ref
  19.7 0.8 copy.32
  20.4 0.7 copy.33.grad_ref
  21.2 0.6 broadcast_in_dim.29.head_ref
  21.8 15.2 %shard_map.175 = (f32[3328,128]{1,0:T(8,128)S(1)}, bf16[128,128]{1,0:T(8,128)(2,1)S(1)}) custom-call(s32[128,128]{1,0:T(8,128)S(1)} %pad.4.ids_ref, bf16[3072,128]{1,0:T(8,128)(2,1)S(1)} %copy-done, bf16[128,13]{1,0:T(8,128)(2,1)S(1)} %copy.31.dense_ref, bf16[13,512]{1,0:T(8,128)(2,1)S(1)} %copy-done.5, bf16[512,256]{1,0:T(8,128)(2,1)S(1)} %copy-done.2, ...), custom_call_target="tpu_custom_call" | custom-call | flops 2617245696 | bytes 4000000 | tf_op jit(solution)/shard_map/pallas_call | solution.py:235
  37.1 1.2 copy-done.8
  38.3 0.6 copy-done.10
  38.9 8.6 %all-to-all-done = bf16[12,256,128]{2,1,0:T(8,128)(2,1)S(1)} async-done(((bf16[12,256,128]{2,1,0:T(8,128)(2,1)}), bf16[12,256,128]{2,1,0:T(8,128)(2,1)S(1)}, u32[]{:S(2)}, u32[]{:S(2)}) %all-to-all-start) | async-done | bytes 786464 | tf_op jit(solution)/shard_map/all_to_all | solution.py:289
  47.6 0.9 copy-done.11
  48.4 16.3 %shard_map.177 = (f32[128,1]{1,0:T(8,128)}, bf16[1664,256]{1,0:T(8,128)(2,1)}, bf16[3072,128]{1,0:T(8,128)(2,1)}) custom-call(f32[3328,128]{1,0:T(8,128)} %copy-done.8, bf16[128,128]{1,0:T(8,128)(2,1)} %copy-done.10, bf16[3072,128]{1,0:T(8,128)(2,1)} %bitcast.21, s32[12,256]{1,0:T(8,128)} %bags_ref.1, s32[256,12]{1,0:T(8,128)} %bitcast.24, ...), custom_call_target="tpu_custom_call" | custom-call | flops 7046430720 | bytes 14000000 | tf_op jit(solution)/shard_map/pallas_call | solution.py:241
  64.8 7.6 %all-to-all-start.1 = ((bf16[12,256,128]{2,1,0:T(8,128)(2,1)}), bf16[12,256,128]{2,1,0:T(8,128)(2,1)S(1)}, u32[]{:S(2)}, u32[]{:S(2)}) async-start(bf16[12,256,128]{2,1,0:T(8,128)(2,1)} %bitcast.20), calls=%async_computation.1 | async-start | bytes 1572864 | tf_op jit(solution)/shard_map/all_to_all | solution.py:289
  72.4 0.0 copy-start.9
  72.4 1.1 copy-done.9
  73.5 5.7 %shard_map.178 = (f32[1536,128]{1,0:T(8,128)S(1)}, bf16[1536,128]{1,0:T(8,128)(2,1)S(1)}) custom-call(s32[1]{0:T(128)} %bitcast.5.core_ref, bf16[1664,256]{1,0:T(8,128)(2,1)S(1)} %copy-done.9, s32[128,52]{1,0:T(8,128)S(1)} %copy.30.ids_ref, s32[52,128]{1,0:T(8,128)S(1)} %bitcast.18), custom_call_target="tpu_custom_call" | custom-call | flops 2617245696 | bytes 3000000 | tf_op jit(solution)/shard_map/pallas_call | solution.py:259
  79.2 0.0 copy-start.16
  79.2 0.0 copy-start.3
  79.3 0.0 copy-start.6
  79.3 0.0 copy-start.7
  79.3 3.1 %collective-permute-start = (bf16[1536,128]{1,0:T(8,128)(2,1)S(1)}, bf16[1536,128]{1,0:T(8,128)(2,1)S(1)}, u32[]{:S(2)}, u32[]{:S(2)}) collective-permute-start(bf16[1536,128]{1,0:T(8,128)(2,1)S(1)} %get-tuple-element.23), channel_id=1, source_target_pairs={{0,12},{12,0},{24,36},{36,24},{48,60},{60,48},{72,84},{84,72},{96,... | collective-permute-start | bytes 1179656 | tf_op jit(solution)/shard_map/ppermute | solution.py:329
  82.4 1.3 collective-permute-done.met_ref
  83.7 0.1 shard_map.179
  83.8 4.4 %collective-permute-start.3 = (bf16[384,128]{1,0:T(8,128)(2,1)S(1)}, bf16[384,128]{1,0:T(8,128)(2,1)S(1)}, u32[]{:S(2)}, u32[]{:S(2)}) collective-permute-start(bf16[384,128]{1,0:T(8,128)(2,1)S(1)} %get-tuple-element.27), channel_id=1, source_target_pairs={{0,576},{12,588},{24,600},{36,612},{48,624},{60,636},{72,648},{84,... | collective-permute-start | bytes 294920 | tf_op jit(solution)/shard_map/ppermute | solution.py:333
  88.2 2.4 %collective-permute-start.2 = (bf16[384,128]{1,0:T(8,128)(2,1)S(1)}, bf16[384,128]{1,0:T(8,128)(2,1)S(1)}, u32[]{:S(2)}, u32[]{:S(2)}) collective-permute-start(bf16[384,128]{1,0:T(8,128)(2,1)S(1)} %get-tuple-element.26), channel_id=1, source_target_pairs={{0,384},{12,396},{24,408},{36,420},{48,432},{60,444},{72,456},{84,... | collective-permute-start | bytes 294920 | tf_op jit(solution)/shard_map/ppermute | solution.py:333
  90.6 2.5 %collective-permute-start.1 = (bf16[384,128]{1,0:T(8,128)(2,1)S(1)}, bf16[384,128]{1,0:T(8,128)(2,1)S(1)}, u32[]{:S(2)}, u32[]{:S(2)}) collective-permute-start(bf16[384,128]{1,0:T(8,128)(2,1)S(1)} %get-tuple-element.25), channel_id=1, source_target_pairs={{0,192},{12,204},{24,216},{36,228},{48,240},{60,252},{72,264},{84,... | collective-permute-start | bytes 294920 | tf_op jit(solution)/shard_map/ppermute | solution.py:333
  93.2 1.9 %collective-permute-done.2 = bf16[384,128]{1,0:T(8,128)(2,1)S(1)} collective-permute-done((bf16[384,128]{1,0:T(8,128)(2,1)S(1)}, bf16[384,128]{1,0:T(8,128)(2,1)S(1)}, u32[]{:S(2)}, u32[]{:S(2)}) %collective-permute-start.2) | collective-permute-done | bytes 98336 | tf_op jit(solution)/shard_map/ppermute | solution.py:333
  95.1 2.3 %collective-permute-done.1 = bf16[384,128]{1,0:T(8,128)(2,1)S(1)} collective-permute-done((bf16[384,128]{1,0:T(8,128)(2,1)S(1)}, bf16[384,128]{1,0:T(8,128)(2,1)S(1)}, u32[]{:S(2)}, u32[]{:S(2)}) %collective-permute-start.1) | collective-permute-done | bytes 98336 | tf_op jit(solution)/shard_map/ppermute | solution.py:333
  97.4 0.1 add_convert_fusion
  97.4 2.8 %all-to-all-done.1 = bf16[12,256,128]{2,1,0:T(8,128)(2,1)S(1)} async-done(((bf16[12,256,128]{2,1,0:T(8,128)(2,1)}), bf16[12,256,128]{2,1,0:T(8,128)(2,1)S(1)}, u32[]{:S(2)}, u32[]{:S(2)}) %all-to-all-start.1) | async-done | bytes 786464 | tf_op jit(solution)/shard_map/all_to_all | solution.py:289
  100.2 14.2 %all_to_all.50 = bf16[8,48,128]{2,1,0:T(8,128)(2,1)S(1)} all-to-all(bf16[8,48,128]{2,1,0:T(8,128)(2,1)S(1)} %bitcast.23), channel_id=1, replica_groups={{0,24,48,72,96,120,144,168},{12,36,60,84,108,132,156,180},{192,216,240,..., dimensions={0} | all-to-all | bytes 196608 | tf_op jit(solution)/shard_map/all_to_all | solution.py:289
  114.4 0.7 broadcast_in_dim.32
  115.1 7.7 %all-to-all-start.3 = ((bf16[12,48,128]{2,1,0:T(8,128)(2,1)}), bf16[12,48,128]{2,1,0:T(8,128)(2,1)S(1)}, u32[]{:S(2)}, u32[]{:S(2)}) async-start(bf16[12,48,128]{2,1,0:T(8,128)(2,1)} %broadcast_in_dim.32), calls=%async_computation.3 | async-start | bytes 294912 | tf_op jit(solution)/shard_map/all_to_all | solution.py:289
  122.8 0.1 copy.35.accum_ref
  123.0 2.7 %shard_map.180 = f32[512,128]{1,0:T(8,128)} custom-call(s32[1,12]{1,0:T(1,128)S(1)} %copy-done.7, s32[12,256]{1,0:T(8,128)S(1)} %copy-done.6, bf16[3072,128]{1,0:T(8,128)(2,1)S(1)} %bitcast.17, bf16[512,128]{1,0:T(8,128)(2,1)S(1)} %copy-done.3, f32[512,1]{1,0:T(8,128)S(1)} %copy.35.accum_ref), custom_call_target="tpu_custom_call" | custom-call | flops 402653184 | bytes 2000000 | tf_op jit(solution)/shard_map/pallas_call | solution.py:283
  125.7 7.9 %all-to-all-done.3 = bf16[12,48,128]{2,1,0:T(8,128)(2,1)S(1)} async-done(((bf16[12,48,128]{2,1,0:T(8,128)(2,1)}), bf16[12,48,128]{2,1,0:T(8,128)(2,1)S(1)}, u32[]{:S(2)}, u32[]{:S(2)}) %all-to-all-start.3) | async-done | bytes 147488 | tf_op jit(solution)/shard_map/all_to_all | solution.py:289
  133.6 0.1 multiply_reduce_fusion
  133.7 0.8 add_sqrt_fusion
  134.5 0.1 divide_convert_fusion
  134.6 0.1 broadcast_in_dim.34
  134.6 14.8 %all_to_all.51 = bf16[32,48,128]{2,1,0:T(8,128)(2,1)S(1)} all-to-all(bf16[32,48,128]{2,1,0:T(8,128)(2,1)S(1)} %broadcast_in_dim.34), channel_id=1, replica_groups={{0,24,48,72,96,120,144,168,192,216,240,264,288,312,336,360,384,408,432,..., dimensions={0} | all-to-all | bytes 786432 | tf_op jit(solution)/shard_map/all_to_all | solution.py:289
  149.5 8.5 %collective-permute-start.4 = (bf16[1536,128]{1,0:T(8,128)(2,1)S(1)}, bf16[1536,128]{1,0:T(8,128)(2,1)S(1)}, u32[]{:S(2)}, u32[]{:S(2)}) collective-permute-start(bf16[1536,128]{1,0:T(8,128)(2,1)S(1)} %bitcast.19), channel_id=1, source_target_pairs={{0,12},{12,0},{24,36},{36,24},{48,60},{60,48},{72,84},{84,72},{96,... | collective-permute-start | bytes 1179656 | tf_op jit(solution)/shard_map/ppermute | solution.py:347
  158.0 0.6 reduce.2
  158.6 0.7 collective-permute-done.4
  159.3 0.1 broadcast_select_fusion.1
  159.4 1.3 convert_subtract_fusion
  (30 shorter events, 0.1 us)
Async XLA Ops:
  0.6 18.8 %copy-start.1 = (s32[128,52]{0,1:T(8,128)S(1)}, s32[128,52]{0,1:T(8,128)}, u32[]{:S(2)}) copy-start(s32[128,52]{0,1:T(8,128)} %param.17) | copy-start | bytes 79876
  0.6 18.9 %copy-start.15 = (bf16[128,13]{0,1:T(8,128)(2,1)S(1)}, bf16[128,13]{0,1:T(8,128)(2,1)}, u32[]{:S(2)}) copy-start(bf16[128,13]{0,1:T(8,128)(2,1)} %param.16) | copy-start | bytes 9988
  0.7 19.0 %copy-start.13 = (s32[12,256]{1,0:T(8,128)S(1)}, s32[12,256]{1,0:T(8,128)}, u32[]{:S(2)}) copy-start(s32[12,256]{1,0:T(8,128)} %bags_ref.1) | copy-start | bytes 36868
  0.7 19.8 %copy-start.17 = (f32[128]{0:T(128)S(1)}, f32[128]{0:T(128)}, u32[]{:S(2)}) copy-start(f32[128]{0:T(128)} %param.18) | copy-start | bytes 1540
  0.7 20.5 %copy-start.14 = (f32[3456]{0:T(1024)S(1)}, f32[3456]{0:T(1024)}, u32[]{:S(2)}) copy-start(f32[3456]{0:T(1024)} %param.31) | copy-start | bytes 41476
  0.7 21.1 %copy-start = (bf16[3072,128]{1,0:T(8,128)(2,1)S(1)}, bf16[3072,128]{1,0:T(8,128)(2,1)}, u32[]{:S(2)}) copy-start(bf16[3072,128]{1,0:T(8,128)(2,1)} %table_ref.3) | copy-start | bytes 2359300
  0.7 21.1 %copy-start.5 = (bf16[13,512]{1,0:T(8,128)(2,1)S(1)}, bf16[13,512]{1,0:T(8,128)(2,1)}, u32[]{:S(2)}) copy-start(bf16[13,512]{1,0:T(8,128)(2,1)} %one_ref.1) | copy-start | bytes 39940
  0.7 21.1 %copy-start.2 = (bf16[512,256]{1,0:T(8,128)(2,1)S(1)}, bf16[512,256]{1,0:T(8,128)(2,1)}, u32[]{:S(2)}) copy-start(bf16[512,256]{1,0:T(8,128)(2,1)} %two_ref.1) | copy-start | bytes 786436
  0.7 21.1 %copy-start.4 = (bf16[256,128]{1,0:T(8,128)(2,1)S(1)}, bf16[256,128]{1,0:T(8,128)(2,1)}, u32[]{:S(2)}) copy-start(bf16[256,128]{1,0:T(8,128)(2,1)} %three_ref.1) | copy-start | bytes 196612
  3.7 43.9 %all-to-all-start = ((bf16[12,256,128]{2,1,0:T(8,128)(2,1)}), bf16[12,256,128]{2,1,0:T(8,128)(2,1)S(1)}, u32[]{:S(2)}, u32[]{:S(2)}) async-start(bf16[12,256,128]{2,1,0:T(8,128)(2,1)} %bitcast.22), calls=%async_computation | async-start | bytes 1572864 | tf_op jit(solution)/shard_map/all_to_all | solution.py:289
  37.1 1.2 copy-start.8
  38.3 0.6 copy-start.10
  47.6 0.9 copy-start.11
  64.8 35.5 %all-to-all-start.1 = ((bf16[12,256,128]{2,1,0:T(8,128)(2,1)}), bf16[12,256,128]{2,1,0:T(8,128)(2,1)S(1)}, u32[]{:S(2)}, u32[]{:S(2)}) async-start(bf16[12,256,128]{2,1,0:T(8,128)(2,1)} %bitcast.20), calls=%async_computation.1 | async-start | bytes 1572864 | tf_op jit(solution)/shard_map/all_to_all | solution.py:289
  72.4 1.2 copy-start.9
  79.2 43.6 %copy-start.16 = (f32[512]{0:T(512)S(1)}, f32[512]{0:T(512)}, u32[]{:S(2)}) copy-start(f32[512]{0:T(512)} %param.22) | copy-start | bytes 6148
  79.2 43.8 %copy-start.3 = (bf16[512,128]{1,0:T(8,128)(2,1)S(1)}, bf16[512,128]{1,0:T(8,128)(2,1)}, u32[]{:S(2)}) copy-start(bf16[512,128]{1,0:T(8,128)(2,1)} %table_ref.5) | copy-start | bytes 393220
  79.3 43.8 %copy-start.6 = (s32[12,256]{1,0:T(8,128)S(1)}, s32[12,256]{1,0:T(8,128)}, u32[]{:S(2)}) copy-start(s32[12,256]{1,0:T(8,128)} %rows_ref.3) | copy-start | bytes 36868
  79.3 43.8 %copy-start.7 = (s32[1,12]{1,0:T(1,128)S(1)}, s32[1,12]{1,0:T(1,128)}, u32[]{:S(2)}) copy-start(s32[1,12]{1,0:T(1,128)} %count_ref.3) | copy-start | bytes 148
  79.3 4.4 %collective-permute-start = (bf16[1536,128]{1,0:T(8,128)(2,1)S(1)}, bf16[1536,128]{1,0:T(8,128)(2,1)S(1)}, u32[]{:S(2)}, u32[]{:S(2)}) collective-permute-start(bf16[1536,128]{1,0:T(8,128)(2,1)S(1)} %get-tuple-element.23), channel_id=1, source_target_pairs={{0,12},{12,0},{24,36},{36,24},{48,60},{60,48},{72,84},{84,72},{96,... | collective-permute-start | bytes 1179656 | tf_op jit(solution)/shard_map/ppermute | solution.py:329
  83.8 9.4 %collective-permute-start.3 = (bf16[384,128]{1,0:T(8,128)(2,1)S(1)}, bf16[384,128]{1,0:T(8,128)(2,1)S(1)}, u32[]{:S(2)}, u32[]{:S(2)}) collective-permute-start(bf16[384,128]{1,0:T(8,128)(2,1)S(1)} %get-tuple-element.27), channel_id=1, source_target_pairs={{0,576},{12,588},{24,600},{36,612},{48,624},{60,636},{72,648},{84,... | collective-permute-start | bytes 294920 | tf_op jit(solution)/shard_map/ppermute | solution.py:333
  88.2 6.9 %collective-permute-start.2 = (bf16[384,128]{1,0:T(8,128)(2,1)S(1)}, bf16[384,128]{1,0:T(8,128)(2,1)S(1)}, u32[]{:S(2)}, u32[]{:S(2)}) collective-permute-start(bf16[384,128]{1,0:T(8,128)(2,1)S(1)} %get-tuple-element.26), channel_id=1, source_target_pairs={{0,384},{12,396},{24,408},{36,420},{48,432},{60,444},{72,456},{84,... | collective-permute-start | bytes 294920 | tf_op jit(solution)/shard_map/ppermute | solution.py:333
  90.6 6.7 %collective-permute-start.1 = (bf16[384,128]{1,0:T(8,128)(2,1)S(1)}, bf16[384,128]{1,0:T(8,128)(2,1)S(1)}, u32[]{:S(2)}, u32[]{:S(2)}) collective-permute-start(bf16[384,128]{1,0:T(8,128)(2,1)S(1)} %get-tuple-element.25), channel_id=1, source_target_pairs={{0,192},{12,204},{24,216},{36,228},{48,240},{60,252},{72,264},{84,... | collective-permute-start | bytes 294920 | tf_op jit(solution)/shard_map/ppermute | solution.py:333
  115.1 18.5 %all-to-all-start.3 = ((bf16[12,48,128]{2,1,0:T(8,128)(2,1)}), bf16[12,48,128]{2,1,0:T(8,128)(2,1)S(1)}, u32[]{:S(2)}, u32[]{:S(2)}) async-start(bf16[12,48,128]{2,1,0:T(8,128)(2,1)} %broadcast_in_dim.32), calls=%async_computation.3 | async-start | bytes 294912 | tf_op jit(solution)/shard_map/all_to_all | solution.py:289
  122.8 35.1 %copy-start.12 = (f32[128,1]{1,0:T(8,128)S(1)}, f32[128,1]{1,0:T(8,128)}, u32[]{:S(2)}) copy-start(f32[128,1]{1,0:T(8,128)} %get-tuple-element.20) | copy-start | bytes 1540
  149.5 9.8 %collective-permute-start.4 = (bf16[1536,128]{1,0:T(8,128)(2,1)S(1)}, bf16[1536,128]{1,0:T(8,128)(2,1)S(1)}, u32[]{:S(2)}, u32[]{:S(2)}) collective-permute-start(bf16[1536,128]{1,0:T(8,128)(2,1)S(1)} %bitcast.19), channel_id=1, source_target_pairs={{0,12},{12,0},{24,36},{36,24},{48,60},{60,48},{72,84},{84,72},{96,... | collective-permute-start | bytes 1179656 | tf_op jit(solution)/shard_map/ppermute | solution.py:347
